TPU v7x, 32 devices: a whole 2x2x4 slice. The times are simulated.
32 devices in a mesh: sample: 2 (over core), prefix: 16 (over z, y, x).
Axes of the slice: x: 2, y: 2, z: 4, core: 2. Of those that a mesh axis runs over, the one named last changes fastest.
Arguments:
- resp_q: bfloat16 [32, 128, 4096], P(('sample', 'prefix')), may hold values from -6 to 6
- resp_k: bfloat16 [32, 128, 512], P(('sample', 'prefix')), may hold values from -6 to 6
- resp_v: bfloat16 [32, 128, 512], P(('sample', 'prefix')), may hold values from -6 to 6
- resp_do: bfloat16 [32, 128, 4096], P(('sample', 'prefix')), may hold values from -6 to 6
- resp_out: bfloat16 [32, 128, 4096], P(('sample', 'prefix')), may hold values from -6 to 6
- resp_lse: float32 [32, 128, 32], P(('sample', 'prefix'))
- prompt_k: bfloat16 [256, 512], P('prefix'), may hold values from -6 to 6
- prompt_v: bfloat16 [256, 512], P('prefix'), may hold values from -6 to 6
- resp_lengths: int32 [32], P(('sample', 'prefix')), may hold values from 16 to 128, as said below
Outputs:
- resp_dq: bfloat16 [32, 128, 4096], P(('sample', 'prefix'))
- resp_dk: bfloat16 [32, 128, 512], P(('sample', 'prefix'))
- resp_dv: bfloat16 [32, 128, 512], P(('sample', 'prefix'))
- prompt_dk: float32 [256, 512], P('prefix')
- prompt_dv: float32 [256, 512], P('prefix')
Inputs may be any that keep to these rules, and one draw needn't show every extreme that they name: `resp_lengths`: some response has exactly 128 live tokens and some has 16.
All inputs are finite; a program needn't handle non-finite values.
Results may differ from a plain program's by a relative error of at most 0.0051.
Values may be sent and summed in bfloat16 or wider, within the bound.
A program may use at most 64 MiB of HBM per device.

v0:
```python
import jax
import jax.numpy as jnp
from jax import lax
from jax.sharding import PartitionSpec as P

H = 32
KVH = 4
HD = 128


def block_size(total_rows):
    return max((size for size in range(1, min(total_rows, 256) + 1) if total_rows % size == 0))


def body(resp_q, resp_k, resp_v, resp_do, resp_out, resp_lse, prompt_k, prompt_v, resp_lengths):
    pair_count, row_count, _ = resp_q.shape
    groups = H // KVH
    kv_width = KVH * HD
    score_scale = HD ** (-0.5)
    shard_count = lax.axis_size("prefix")
    query_pos = jnp.arange(row_count, dtype=jnp.int32)
    live_rows = query_pos[None, :] < resp_lengths[:, None]
    query_heads = resp_q.reshape(pair_count, row_count, KVH, groups, HD)
    grad_heads = resp_do.reshape(pair_count, row_count, KVH, groups, HD)
    out_heads = resp_out.reshape(pair_count, row_count, KVH, groups, HD)
    out_dot = jnp.sum(grad_heads.astype(jnp.float32) * out_heads.astype(jnp.float32), -1)
    dot_cols = out_dot.transpose(0, 2, 3, 1)[..., None]
    lse_cols = resp_lse.reshape(pair_count, row_count, KVH, groups).transpose(0, 2, 3, 1)[..., None]

    def key_block(block_keys, block_values, live_mask, shared):
        key_form = "ukd" if shared else "bukd"
        key_heads = block_keys.reshape(block_keys.shape[:-1] + (KVH, HD))
        value_heads = block_values.reshape(block_values.shape[:-1] + (KVH, HD))
        scores = (
            jnp.einsum(
                "btkgd," + key_form + "->bkgtu",
                query_heads,
                key_heads,
                preferred_element_type=jnp.float32,
            )
            * score_scale
        )
        probs = jnp.exp(scores - lse_cols) * live_mask[:, None, None].astype(jnp.float32)
        prob_grad = jnp.einsum(
            "btkgd," + key_form + "->bkgtu",
            grad_heads,
            value_heads,
            preferred_element_type=jnp.float32,
        )
        score_grad = probs * (prob_grad - dot_cols)
        probs_low = probs.astype(jnp.bfloat16)
        score_low = score_grad.astype(jnp.bfloat16)
        query_grad = (
            jnp.einsum(
                "bkgtu," + key_form + "->btkgd",
                score_low,
                key_heads,
                preferred_element_type=jnp.float32,
            )
            * score_scale
        )
        key_grad = (
            jnp.einsum(
                "bkgtu,btkgd->" + key_form,
                score_low,
                query_heads,
                preferred_element_type=jnp.float32,
            )
            * score_scale
        )
        value_grad = jnp.einsum(
            "bkgtu,btkgd->" + key_form, probs_low, grad_heads, preferred_element_type=jnp.float32
        )
        both_grads = jnp.concatenate(
            [
                key_grad.reshape(key_grad.shape[:-2] + (kv_width,)),
                value_grad.reshape(value_grad.shape[:-2] + (kv_width,)),
            ],
            -1,
        )
        return (query_grad, both_grads)

    prompt_total = prompt_k.shape[0] * shard_count
    query_zero = jnp.zeros((pair_count, row_count, KVH, groups, HD), jnp.float32)
    prompt_zero = jnp.zeros((prompt_total, 2 * kv_width), jnp.float32)
    pieces = (
        lax.all_gather(prompt_k, "prefix", axis=0, tiled=True),
        lax.all_gather(prompt_v, "prefix", axis=0, tiled=True),
    )
    piece_rows = pieces[0].shape[0]
    prompt_size = block_size(piece_rows)
    count = piece_rows // prompt_size
    keys_split = pieces[0].reshape(count, prompt_size, kv_width)
    values_split = pieces[1].reshape(count, prompt_size, kv_width)
    live_mask = jnp.broadcast_to(live_rows[:, :, None], (pair_count, row_count, prompt_size))

    def inner(query_acc, items):
        query_grad, both_grads = key_block(items[0], items[1], live_mask, True)
        return (query_acc + query_grad, both_grads)

    query_acc, grads = lax.scan(inner, query_zero, (keys_split, values_split))
    grads = grads.reshape(piece_rows, 2 * kv_width)
    query_sum = query_acc
    prompt_terms = lax.dynamic_update_slice_in_dim(prompt_zero, grads, jnp.int32(0), 0)
    size = block_size(row_count)
    count = row_count // size
    keys_split = resp_k.reshape(pair_count, count, size, kv_width).transpose(1, 0, 2, 3)
    values_split = resp_v.reshape(pair_count, count, size, kv_width).transpose(1, 0, 2, 3)
    block_index = jnp.arange(count, dtype=jnp.int32)

    def own_step(query_acc, items):
        key_pos = items[2] * size + jnp.arange(size, dtype=jnp.int32)
        live_mask = (key_pos[None, None, :] <= query_pos[None, :, None]) & live_rows[:, :, None]
        query_grad, both_grads = key_block(items[0], items[1], live_mask, False)
        return (query_acc + query_grad, both_grads)

    query_sum, own_terms = lax.scan(own_step, query_sum, (keys_split, values_split, block_index))
    own_grads = own_terms.transpose(1, 0, 2, 3).reshape(pair_count, row_count, 2 * kv_width)
    resp_dq = query_sum.reshape(pair_count, row_count, H * HD).astype(jnp.bfloat16)
    resp_dk = own_grads[..., :kv_width].astype(jnp.bfloat16)
    resp_dv = own_grads[..., kv_width:].astype(jnp.bfloat16)
    local_sum = lax.psum_scatter(prompt_terms, "prefix", scatter_dimension=0, tiled=True)
    prompt_grads = lax.psum(local_sum, "sample")
    return (resp_dq, resp_dk, resp_dv, prompt_grads[:, :kv_width], prompt_grads[:, kv_width:])


def solution(mesh):
    return jax.shard_map(
        body,
        mesh=mesh,
        in_specs=(
            P(("sample", "prefix"), None, None),
            P(("sample", "prefix"), None, None),
            P(("sample", "prefix"), None, None),
            P(("sample", "prefix"), None, None),
            P(("sample", "prefix"), None, None),
            P(("sample", "prefix"), None, None),
            P("prefix", None),
            P("prefix", None),
            P(("sample", "prefix")),
        ),
        out_specs=(
            P(("sample", "prefix"), None, None),
            P(("sample", "prefix"), None, None),
            P(("sample", "prefix"), None, None),
            P("prefix", None),
            P("prefix", None),
        ),
        check_vma=False,
    )
```

profile of v0, /device:TPU:0, one launch (start us, length us, event | category | flops | bytes accessed | tf_op | source)
XLA Modules:
  0.0 211.3 jit_solution(9231339018671859267)
XLA Ops:
  7.2 0.0 copy-start.9
  7.2 0.0 copy-start.3
  7.2 0.0 reduce-scatter.2.cloned.1.call-start
  7.2 1.7 copy.117
  8.9 0.0 copy-done.9
  8.9 43.8 %all_gather.6 = bf16[256,512]{1,0:T(8,128)(2,1)S(1)} all-gather(bf16[16,512]{1,0:T(8,128)(2,1)S(1)} %copy-done.9), channel_id=1, replica_groups=mesh['sample'=2,'prefix'=16] {'prefix'}, dimensions={0}, use_global_device_ids=true | all-gather | bytes 278528 | tf_op jit(solution)/shard_map/all_gather | solution.py:87
  52.7 0.1 copy.63
  52.9 0.0 copy-done.3
  52.9 0.7 copy.118
  53.5 0.0 copy-start
  54.2 1.5 multiply_bitcast_fusion
  55.7 1.7 copy.119
  57.4 0.0 copy-start.10
  57.4 2.3 %reduce_sum.11 = f32[128,4,8]{2,1,0:T(4,128)S(1)} reduce(f32[128,4,8,128]{3,2,1,0:T(8,128)} %bitcast.172, f32[]{:T(128)} %constant.24.clone.1), dimensions={3}, to_apply=%region_0.0 | reduce | flops 520192 | bytes 2113540 | tf_op jit(solution)/shard_map/reduce_sum | solution.py:26
  59.7 0.1 copy.69
  59.8 0.0 copy-done.10
  59.8 36.9 %all_gather.7 = bf16[256,512]{1,0:T(8,128)(2,1)S(1)} all-gather(bf16[16,512]{1,0:T(8,128)(2,1)S(1)} %copy-done.10), channel_id=1, replica_groups=mesh['sample'=2,'prefix'=16] {'prefix'}, dimensions={0}, use_global_device_ids=true | all-gather | bytes 278528 | tf_op jit(solution)/shard_map/all_gather | solution.py:88
  96.6 0.8 copy.66
  97.5 0.0 copy-start.8
  97.5 0.7 fusion.38
  98.2 0.0 copy-done
  98.2 0.0 copy-done.8
  98.2 0.0 copy-start.4
  98.2 1.9 fusion.6
  100.1 0.0 copy-done.4
  100.1 2.6 %fusion.1 = bf16[1,4,8,128,256]{3,4,2,1,0:T(8,128)(2,1)S(1)} fusion(f32[4,256,128,8]{2,1,3,0:T(8,128)S(1)} %fusion.38, bf16[256,4,128,1]{0,2,3,1:T(8,128)(2,1)S(1)} %bitcast.177, bf16[128,4,8,128]{0,3,2,1:T(8,128)(2,1)} %bitcast.169, f32[4,8,128]{2,1,0:T(8,128)S(1)} %copy.69, f32[128]{0:T(128)S(1)} %fusion.36, f32[4,8,128]{2,1,0:T(8,128)S(1)} %bitcast.186), kind=kOutput, calls=%fused_computation.2 | convolution fusion | flops 274726912 | bytes 7635456 | tf_op jit(solution)/shard_map/while/body/eval_jaxpr/btkgd,ukd->bkgtu/dot_general | solution.py:44
  102.7 1.6 fusion.24
  104.3 2.1 copy.86
  106.4 0.0 copy-start.7
  106.4 2.1 copy.87
  108.5 2.3 %pad_maximum_fusion = f32[256,1024]{1,0:T(8,128)} fusion(f32[256,512]{1,0:T(8,128)} %copy.87, f32[256,512]{1,0:T(8,128)} %copy.86), kind=kLoop, calls=%fused_computation.33 | loop fusion | flops 262144 | bytes 2097152 | tf_op jit(solution)/shard_map/while/body/eval_jaxpr/concatenate | solution.py:74
  110.7 0.0 reduce-scatter.2.cloned.1.call-update
  110.7 0.0 all-reduce.2.cloned.1.call-start
  110.8 0.0 copy-done.7
  110.8 0.7 reshape.283
  111.5 1.0 copy.98
  112.5 1.6 reshape.284
  114.1 0.0 copy-start.1
  114.1 0.0 copy-start.6
  114.2 1.4 fusion.12
  115.6 0.0 copy-done.1
  115.6 0.0 copy-done.6
  115.6 0.4 fusion.20
  116.0 0.0 copy-start.2
  116.0 1.1 fusion.29
  117.1 0.5 fusion.15
  117.6 0.0 copy-done.2
  117.6 0.5 fusion.8
  118.1 68.4 %reduce-scatter.2.cloned.1.call-done = f32[16,1024]{1,0:T(8,128)} async-done(((f32[256,1024]{1,0:T(8,128)}), f32[16,1024]{1,0:T(8,128)}) %reduce-scatter.2.cloned.1.call-update) | async-done | bytes 65552 | tf_op jit(solution)/shard_map/reduce_scatter | solution.py:122
  186.6 0.0 all-reduce.2.cloned.1.call-update
  186.6 0.0 copy-start.5
  186.6 1.7 fusion.28
  188.3 1.3 copy.88
  189.6 0.8 copy.89
  190.4 0.0 copy-done.5
  190.4 0.8 copy.90
  191.2 11.9 %all-reduce.2.cloned.1.call-done = f32[16,1024]{1,0:T(8,128)} async-done(((f32[16,1024]{1,0:T(8,128)}), f32[16,1024]{1,0:T(8,128)}) %all-reduce.2.cloned.1.call-update) | async-done | bytes 65552 | tf_op jit(solution)/shard_map/psum | solution.py:123
  203.1 1.4 fusion.37
  (3 shorter events, 0.0 us)
Async XLA Ops:
  7.2 1.8 copy-start.9
  7.2 45.7 %copy-start.3 = (bf16[1,128,4096]{2,1,0:T(8,128)(2,1)S(1)}, bf16[1,128,4096]{2,1,0:T(8,128)(2,1)}, u32[]{:S(2)}) copy-start(bf16[1,128,4096]{2,1,0:T(8,128)(2,1)} %param.12) | copy-start | bytes 3145732
  7.2 179.4 %reduce-scatter.2.cloned.1.call-start = ((), (), s32[]{:S(2)}) async-start(), calls=%async_computation.1 | async-start | bytes 1114112 | tf_op jit(solution)/shard_map/reduce_scatter | solution.py:122
  53.5 44.7 %copy-start = (bf16[1,128,4096]{1,2,0:T(8,128)(2,1)}, bf16[1,128,4096]{1,2,0:T(8,128)(2,1)S(1)}, u32[]{:S(2)}) copy-start(bf16[1,128,4096]{1,2,0:T(8,128)(2,1)S(1)} %copy.118) | copy-start | bytes 3145732
  57.4 2.4 %copy-start.10 = (bf16[16,512]{1,0:T(8,128)(2,1)S(1)}, bf16[16,512]{1,0:T(8,128)(2,1)}, u32[]{:S(2)}) copy-start(bf16[16,512]{1,0:T(8,128)(2,1)} %param.16) | copy-start | bytes 49156
  97.5 0.8 copy-start.8
  98.2 1.9 copy-start.4
  106.4 4.4 %copy-start.7 = (bf16[1,128,512]{2,1,0:T(8,128)(2,1)S(1)}, bf16[1,128,512]{2,1,0:T(8,128)(2,1)}, u32[]{:S(2)}) copy-start(bf16[1,128,512]{2,1,0:T(8,128)(2,1)} %param.10) | copy-start | bytes 393220
  110.7 92.3 %all-reduce.2.cloned.1.call-start = ((), (), s32[]{:S(2)}) async-start(), calls=%async_computation.2 | async-start | bytes 131072 | tf_op jit(solution)/shard_map/psum | solution.py:123
  114.1 1.4 copy-start.1
  114.1 1.4 copy-start.6
  116.0 1.6 copy-start.2
  186.6 3.8 %copy-start.5 = (bf16[4,128,128]{1,2,0:T(8,128)(2,1)S(1)}, bf16[4,128,128]{1,2,0:T(8,128)(2,1)}, u32[]{:S(2)}) copy-start(bf16[4,128,128]{1,2,0:T(8,128)(2,1)} %fusion.29) | copy-start | bytes 393220
Sparse Core Ops, SparseCore 0:
  110.9 75.6 reduce-scatter.1
  189.0 14.0 all-reduce.1
where the time goes:
time: 212 us; the launch traced here: 211 us
  blocking collectives  80.6 us (38%)
  waiting for transfers between devices  80.4 us (38%)
  local copies, waits for them, and re-layouts  16.9 us (8%)
  between operations  14.9 us (7%)
  matrix products  12.4 us (6%)
  other arithmetic  6.04 us (3%)
    reduce_scatter x1, waiting for transfers between devices, body(): lax.psum_scatter(prompt_terms, 'prefix', scatter_dimension=0, tiled=True)  68.4 us
    all_gather x1, blocking collectives, body(): lax.all_gather(prompt_k, 'prefix', axis=0, tiled=True)  43.8 us
    all_gather x1, blocking collectives, body(): lax.all_gather(prompt_v, 'prefix', axis=0, tiled=True)  36.9 us
    psum x1, waiting for transfers between devices, body(): prompt_grads = lax.psum(local_sum, 'sample')  11.9 us
    another operation x5, local copies, waits for them, and re-layouts  5.68 us
    unnamed x26, local copies, waits for them, and re-layouts  4.61 us
  transfers between devices with their start and end apart: 2, of which 2 were waited for; matrix products, arithmetic and copies ran while one was open for 6% of the time, Pallas kernels for 0%

commit v1 on v0

v1 whole, which is shorter than its diff:
```python
import functools
import math

import jax
import jax.numpy as jnp
from jax import lax
from jax.experimental import pallas as pl
from jax.experimental.pallas import tpu as pltpu
from jax.sharding import PartitionSpec as P

H = 32
KVH = 4
HD = 128
G = H // KVH
MESH = pl.DeviceIdType.MESH
NT = (((1,), (1,)), ((), ()))
LOG2E = math.log2(math.e)
SCALE = HD ** (-0.5)
UB = 256


def dot(a, b):
    return jnp.dot(a, b, preferred_element_type=jnp.float32)


def dot_nt(a, b):
    return lax.dot_general(a, b, NT, preferred_element_type=jnp.float32)


def heads_to_rows(block):
    return jnp.concatenate([block[:, g * HD : (g + 1) * HD] for g in range(G)], 0)


def rows_to_lanes(block):
    return jnp.concatenate([block[g : g + 1] for g in range(G)], 1)


def part_grads(keys, values, queries, grads, lse_row, delta_row, live):
    scores = dot_nt(keys, queries)
    probs = jnp.exp2(scores * (SCALE * LOG2E) - lse_row)
    if live is not None:
        probs = jnp.where(live, probs, 0.0)
    prob_grad = dot_nt(values, grads)
    score_low = (probs * (prob_grad - delta_row)).astype(jnp.bfloat16)
    probs_low = probs.astype(jnp.bfloat16)
    dq_t = dot(keys.T, score_low)
    dk = dot(score_low, queries) * SCALE
    dv = dot(probs_low, grads)
    return dq_t, dk, dv


def kernel(
    n, ns, rows, length_ref, q_hbm, k_hbm, v_hbm, do_hbm, out_hbm, lse_hbm, pk_hbm, pv_hbm,
    dq_hbm, dk_ref, dv_ref, pdk_ref, pdv_ref,
    q_ref, k_ref, v_ref, do_ref, out_ref, lse_ref, pk_ref, pv_ref, dq_ref, lse_t, delta_t, dq_acc,
    gathered, parts, landed, totals,
    load_sem, store_sem, gather_send, gather_recv, part_send, part_recv, total_send, total_recv,
):
    tokens = q_ref.shape[0]
    me = lax.axis_index("prefix")
    mine = lax.axis_index("sample")

    pairs = [
        (pk_hbm, pk_ref), (pv_hbm, pv_ref), (do_hbm.at[0], do_ref), (out_hbm.at[0], out_ref),
        (lse_hbm.at[0], lse_ref), (q_hbm.at[0], q_ref), (k_hbm.at[0], k_ref), (v_hbm.at[0], v_ref),
    ]
    loads = [pltpu.make_async_copy(a, b, load_sem.at[i]) for i, (a, b) in enumerate(pairs)]
    for copy in loads:
        copy.start()

    barrier = pltpu.get_barrier_semaphore()

    def greet(d, _):
        pl.semaphore_signal(
            barrier, inc=1, device_id={"prefix": lax.rem(me + d, n)}, device_id_type=MESH
        )
        return 0

    def greet_sample(d, _):
        pl.semaphore_signal(
            barrier, inc=1, device_id={"sample": lax.rem(mine + d, ns)}, device_id_type=MESH
        )
        return 0

    lax.fori_loop(1, n, greet, 0)
    lax.fori_loop(1, ns, greet_sample, 0)
    loads[0].wait()
    loads[1].wait()
    width = KVH * HD
    gathered[0:rows, :width] = pk_ref[...]
    gathered[0:rows, width:] = pv_ref[...]
    pl.semaphore_wait(barrier, n - 1 + ns - 1)

    def gather_copy(d):
        return pltpu.make_async_remote_copy(
            src_ref=gathered.at[pl.ds(0, rows)],
            dst_ref=gathered.at[pl.ds(pl.multiple_of(d * rows, rows), rows)],
            send_sem=gather_send.at[d],
            recv_sem=gather_recv.at[d],
            device_id={"prefix": lax.rem(me + d, n)},
            device_id_type=MESH,
        )

    def start_gather(d, _):
        gather_copy(d).start()
        return 0

    lax.fori_loop(1, n, start_gather, 0)

    for copy in loads[2:]:
        copy.wait()
    length = length_ref[0]
    key_pos = lax.broadcasted_iota(jnp.int32, (tokens, tokens), 0)
    query_pos = lax.broadcasted_iota(jnp.int32, (tokens, tokens), 1)
    causal = key_pos <= query_pos
    live_t = lax.broadcasted_iota(jnp.int32, (H, tokens), 1) < length
    lse_t[...] = jnp.where(live_t, lse_ref[...].T * LOG2E, 1e30)

    def own_step(j, _):
        cols = pl.ds(pl.multiple_of(j * G * HD, G * HD), G * HD)
        head = pl.ds(pl.multiple_of(j * HD, HD), HD)
        stat = pl.ds(pl.multiple_of(j * G, G), G)
        queries = heads_to_rows(q_ref[:, cols])
        grads = heads_to_rows(do_ref[:, cols])
        outs = heads_to_rows(out_ref[:, cols])
        product = grads.astype(jnp.float32) * outs.astype(jnp.float32)
        high = product.astype(jnp.bfloat16)
        low = (product - high.astype(jnp.float32)).astype(jnp.bfloat16)
        ones = jnp.ones((G, HD), jnp.bfloat16)
        sums = dot_nt(ones, high) + dot_nt(ones, low)
        delta_row = sums[0:1]
        for g in range(G):
            delta_t[j, g : g + 1, :] = delta_row[:, g * HD : (g + 1) * HD]
        lse_row = rows_to_lanes(lse_t[stat, :])
        live = jnp.concatenate([causal] * G, 1)
        dq_t, dk, dv = part_grads(
            k_ref[:, head], v_ref[:, head], queries, grads, lse_row, delta_row, live
        )
        dq_acc[j] = dq_t
        dk_ref[0, :, head] = dk.astype(jnp.bfloat16)
        dv_ref[0, :, head] = dv.astype(jnp.bfloat16)
        return 0

    lax.fori_loop(0, KVH, own_step, 0)

    def wait_gather(d, _):
        gather_copy(d).wait()
        return 0

    lax.fori_loop(1, n, wait_gather, 0)

    def part_copy(j, d):
        return pltpu.make_async_remote_copy(
            src_ref=parts.at[j, d],
            dst_ref=landed.at[j, d],
            send_sem=part_send.at[j, d],
            recv_sem=part_recv.at[j, d],
            device_id={"prefix": lax.rem(me + n - d, n)},
            device_id_type=MESH,
        )

    prompt_rows = n * rows
    block = UB if prompt_rows % UB == 0 else prompt_rows

    def prompt_step(j, _):
        cols = pl.ds(pl.multiple_of(j * G * HD, G * HD), G * HD)
        head = pl.ds(pl.multiple_of(j * HD, HD), HD)
        head_v = pl.ds(pl.multiple_of(j * HD + width, HD), HD)
        stat = pl.ds(pl.multiple_of(j * G, G), G)
        queries = heads_to_rows(q_ref[:, cols])
        grads = heads_to_rows(do_ref[:, cols])
        lse_row = rows_to_lanes(lse_t[stat, :])
        delta_row = rows_to_lanes(delta_t[j])

        def block_step(b, _):
            at = pl.ds(pl.multiple_of(b * block, block), block)
            dq_t, dk, dv = part_grads(
                gathered[at, head], gathered[at, head_v], queries, grads, lse_row, delta_row, None
            )
            dq_acc[j] += dq_t
            both = jnp.concatenate([dk, dv], 1).astype(jnp.bfloat16)
            slots = pl.ds(b * (block // rows), block // rows)
            parts[j, slots] = both.reshape(block // rows, rows, 2 * HD)
            return 0

        if prompt_rows == block:
            block_step(0, 0)
        else:
            lax.fori_loop(0, prompt_rows // block, block_step, 0)

        def start_part(d, _):
            part_copy(j, d).start()
            return 0

        lax.fori_loop(1, n, start_part, 0)
        landed[j, 0] = parts[j, 0]
        dq_t = (dq_acc[j] * SCALE).astype(jnp.bfloat16)
        for g in range(G):
            at = pl.ds(pl.multiple_of((j * G + g) * HD, HD), HD)
            dq_ref[:, at] = dq_t[:, g * HD : (g + 1) * HD].T
        return 0

    lax.fori_loop(0, KVH, prompt_step, 0)
    store = pltpu.make_async_copy(dq_ref, dq_hbm.at[0], store_sem)
    store.start()

    def sum_step(j, _):
        def wait_part(d, _):
            part_copy(j, d).wait()
            return 0

        lax.fori_loop(1, n, wait_part, 0)
        totals[mine, j] = jnp.sum(landed[j].astype(jnp.float32), 0)
        return 0

    lax.fori_loop(0, KVH, sum_step, 0)

    def total_copy(d):
        return pltpu.make_async_remote_copy(
            src_ref=totals.at[mine],
            dst_ref=totals.at[mine],
            send_sem=total_send.at[d],
            recv_sem=total_recv.at[d],
            device_id={"sample": lax.rem(mine + d, ns)},
            device_id_type=MESH,
        )

    for d in range(1, ns):
        total_copy(d).start()
    for d in range(1, ns):
        total_copy(d).wait()
    for j in range(KVH):
        both = totals[0, j]
        for s in range(1, ns):
            both = both + totals[s, j]
        pdk_ref[:, j * HD : (j + 1) * HD] = both[:, :HD]
        pdv_ref[:, j * HD : (j + 1) * HD] = both[:, HD:]
    store.wait()


def body(resp_q, resp_k, resp_v, resp_do, resp_out, resp_lse, prompt_k, prompt_v, resp_lengths):
    n = lax.axis_size("prefix")
    ns = lax.axis_size("sample")
    rows, width = prompt_k.shape
    _, tokens, q_width = resp_q.shape
    bf16, f32 = jnp.bfloat16, jnp.float32
    vmem = pl.BlockSpec(memory_space=pltpu.VMEM)
    hbm = pl.BlockSpec(memory_space=pl.ANY)
    dma = pltpu.SemaphoreType.DMA
    return pl.pallas_call(
        functools.partial(kernel, n, ns, rows),
        out_shape=(
            jax.ShapeDtypeStruct(resp_q.shape, bf16),
            jax.ShapeDtypeStruct(resp_k.shape, bf16),
            jax.ShapeDtypeStruct(resp_v.shape, bf16),
            jax.ShapeDtypeStruct((rows, width), f32),
            jax.ShapeDtypeStruct((rows, width), f32),
        ),
        in_specs=[pl.BlockSpec(memory_space=pltpu.SMEM)] + [hbm] * 8,
        out_specs=(hbm, vmem, vmem, vmem, vmem),
        scratch_shapes=[
            pltpu.VMEM((tokens, q_width), bf16),
            pltpu.VMEM((tokens, width), bf16),
            pltpu.VMEM((tokens, width), bf16),
            pltpu.VMEM((tokens, q_width), bf16),
            pltpu.VMEM((tokens, q_width), bf16),
            pltpu.VMEM((tokens, H), f32),
            pltpu.VMEM((rows, width), bf16),
            pltpu.VMEM((rows, width), bf16),
            pltpu.VMEM((tokens, q_width), bf16),
            pltpu.VMEM((H, tokens), f32),
            pltpu.VMEM((KVH, G, tokens), f32),
            pltpu.VMEM((KVH, HD, G * tokens), f32),
            pltpu.VMEM((n * rows, 2 * width), bf16),
            pltpu.VMEM((KVH, n, rows, 2 * HD), bf16),
            pltpu.VMEM((KVH, n, rows, 2 * HD), bf16),
            pltpu.VMEM((ns, KVH, rows, 2 * HD), f32),
            dma((8,)),
            dma(()),
            dma((n,)),
            dma((n,)),
            dma((KVH, n)),
            dma((KVH, n)),
            dma((ns,)),
            dma((ns,)),
        ],
        compiler_params=pltpu.CompilerParams(
            collective_id=0, has_side_effects=True, vmem_limit_bytes=48 * 1024 * 1024
        ),
        cost_estimate=pl.CostEstimate(
            flops=2_000_000_000, bytes_accessed=5_000_000, transcendentals=1_600_000
        ),
    )(resp_lengths, resp_q, resp_k, resp_v, resp_do, resp_out, resp_lse, prompt_k, prompt_v)


def solution(mesh):
    rows = P(("sample", "prefix"), None, None)
    prompt = P("prefix", None)
    return jax.shard_map(
        body,
        mesh=mesh,
        in_specs=(rows, rows, rows, rows, rows, rows, prompt, prompt, P(("sample", "prefix"))),
        out_specs=(rows, rows, rows, prompt, prompt),
        check_vma=False,
    )
```

time: 212 us -> 51.2 us (0.24)
  blocking collectives: 80.6 us -> 0 us
  waiting for transfers between devices: 80.4 us -> 0 us
  Pallas kernels: 0 us -> 39.7 us
  between operations: 14.9 us -> 1.33 us
  matrix products: 12.4 us -> 0 us
  local copies, waits for them, and re-layouts: 16.9 us -> 9.82 us
  other arithmetic: 6.04 us -> 0 us
    all_gather x2 -> x0, blocking collectives: 80.6 us -> none  [the longest x1 43.8 us: body(): lax.all_gather(prompt_k, 'prefix', axis=0, tiled=True)]
    reduce_scatter x1 -> x0, waiting for transfers between devices: 68.4 us -> none  [body(): lax.psum_scatter(prompt_terms, 'prefix', scatter_dimension=0, tiled=True)]
    pallas_call x0 -> x1, Pallas kernels: none -> 39.7 us  [body(): pl.pallas_call(functools.partial(kernel, n, ns, rows), out_shape=(jax.Sha...]
    dot_general x10 -> x0, matrix products: 12.4 us -> none  [the longest x2 3.29 us: key_block(): jnp.einsum('bkgtu,btkgd->' + key_form, score_low, query_heads, preferred_...]
    psum x1 -> x0, waiting for transfers between devices: 11.9 us -> none  [body(): prompt_grads = lax.psum(local_sum, 'sample')]
    another operation x5 -> x0, local copies, waits for them, and re-layouts: 5.68 us -> none
    unnamed x26 -> x20, local copies, waits for them, and re-layouts: 4.61 us -> 9.82 us
    reshape x2 -> x0, local copies, waits for them, and re-layouts: 4.13 us -> none  [the longest x1 2.06 us: key_block(): value_grad.reshape(value_grad.shape[:-2] + (kv_width,))]
  transfers between devices with their start and end apart: 2 -> 0, of which waited for: 2 -> 0; matrix products, arithmetic and copies ran while one was open for 6% -> 0% of each run, Pallas kernels for 0% -> 0%
where the time goes in v1:
time: 51.2 us; the launch traced here: 50.9 us
  Pallas kernels  39.7 us (78%)
  local copies, waits for them, and re-layouts  9.82 us (19%)
  between operations  1.33 us (3%)
    pallas_call x1, Pallas kernels, body(): pl.pallas_call(functools.partial(kernel, n, ns, rows), out_shape=(jax.Sha...  39.7 us
    unnamed x20, local copies, waits for them, and re-layouts  9.82 us

profile of v1, /device:TPU:0, one launch (start us, length us, event | category | flops | bytes accessed | tf_op | source)
XLA Modules:
  0.0 50.9 jit_solution(8876343690303732894)
XLA Ops:
  1.3 0.0 copy-start.5
  1.3 0.0 copy-start.6
  1.3 0.8 %copy.14.lse_hbm = f32[1,128,32]{2,1,0:T(8,128)S(1)} copy(f32[1,128,32]{1,2,0:T(8,128)} %param.14) | data formatting | bytes 32768 | tf_op args[5]
  2.1 0.0 copy-done.5
  2.1 0.0 copy-done.6
  2.1 0.0 copy-start
  2.2 1.2 %copy-done = bf16[1,128,4096]{2,1,0:T(8,128)(2,1)S(1)} copy-done((bf16[1,128,4096]{2,1,0:T(8,128)(2,1)S(1)}, bf16[1,128,4096]{2,1,0:T(8,128)(2,1)}, u32[]{:S(2)}) %copy-start) | copy-done | bytes 1048600
  3.4 0.0 copy-start.1
  3.4 1.2 %copy-done.1 = bf16[1,128,4096]{2,1,0:T(8,128)(2,1)S(1)} copy-done((bf16[1,128,4096]{2,1,0:T(8,128)(2,1)S(1)}, bf16[1,128,4096]{2,1,0:T(8,128)(2,1)}, u32[]{:S(2)}) %copy-start.1) | copy-done | bytes 1048600
  4.6 0.0 copy-start.2
  4.6 1.2 %copy-done.2 = bf16[1,128,4096]{2,1,0:T(8,128)(2,1)S(1)} copy-done((bf16[1,128,4096]{2,1,0:T(8,128)(2,1)S(1)}, bf16[1,128,4096]{2,1,0:T(8,128)(2,1)}, u32[]{:S(2)}) %copy-start.2) | copy-done | bytes 1048600
  5.8 0.0 copy-start.3
  5.8 0.9 %copy-done.3 = bf16[1,128,512]{2,1,0:T(8,128)(2,1)S(1)} copy-done((bf16[1,128,512]{2,1,0:T(8,128)(2,1)S(1)}, bf16[1,128,512]{2,1,0:T(8,128)(2,1)}, u32[]{:S(2)}) %copy-start.3) | copy-done | bytes 131096
  6.7 0.0 copy-start.4
  6.7 0.9 %copy-done.4 = bf16[1,128,512]{2,1,0:T(8,128)(2,1)S(1)} copy-done((bf16[1,128,512]{2,1,0:T(8,128)(2,1)S(1)}, bf16[1,128,512]{2,1,0:T(8,128)(2,1)}, u32[]{:S(2)}) %copy-start.4) | copy-done | bytes 131096
  7.6 39.7 %shard_map.128 = (bf16[1,128,4096]{2,1,0:T(8,128)(2,1)S(1)}, bf16[1,128,512]{2,1,0:T(8,128)(2,1)S(1)}, bf16[1,128,512]{2,1,0:T(8,128)(2,1)S(1)}, f32[16,512]{1,0:T(8,128)S(1)}, f32[16,512]{1,0:T(8,128)S(1)}) custom-call(s32[1]{0:T(128)S(6)} %copy.20.length_ref, bf16[1,128,4096]{2,1,0:T(8,128)(2,1)S(1)} %copy-done, bf16[1,128,512]{2,1,0:T(8,128)(2,1)S(1)} %copy-done.3, ...), custom_call_target="tpu_custom_call" | custom-call | flops 2000000000 | bytes 5000000 | tf_op jit(solution)/shard_map/pallas_call | solution.py:250
  47.3 1.0 %copy.21 = bf16[1,128,4096]{2,1,0:T(8,128)(2,1)} copy(bf16[1,128,4096]{2,1,0:T(8,128)(2,1)S(1)} %get-tuple-element.10) | data formatting | bytes 2097152
  48.3 0.7 %copy.22 = bf16[1,128,512]{2,1,0:T(8,128)(2,1)} copy(bf16[1,128,512]{2,1,0:T(8,128)(2,1)S(1)} %get-tuple-element.11) | data formatting | bytes 262144
  49.0 0.7 %copy.23 = bf16[1,128,512]{2,1,0:T(8,128)(2,1)} copy(bf16[1,128,512]{2,1,0:T(8,128)(2,1)S(1)} %get-tuple-element.12) | data formatting | bytes 262144
  49.6 0.6 %copy.24 = f32[16,512]{1,0:T(8,128)} copy(f32[16,512]{1,0:T(8,128)S(1)} %get-tuple-element.13) | data formatting | bytes 65536
  50.2 0.6 %copy.25 = f32[16,512]{1,0:T(8,128)} copy(f32[16,512]{1,0:T(8,128)S(1)} %get-tuple-element.14) | data formatting | bytes 65536
Async XLA Ops:
  1.3 0.8 %copy-start.5 = (bf16[16,512]{1,0:T(8,128)(2,1)S(1)}, bf16[16,512]{1,0:T(8,128)(2,1)}, u32[]{:S(2)}) copy-start(bf16[16,512]{1,0:T(8,128)(2,1)} %pk_hbm.1) | copy-start | bytes 49156
  1.3 0.8 %copy-start.6 = (bf16[16,512]{1,0:T(8,128)(2,1)S(1)}, bf16[16,512]{1,0:T(8,128)(2,1)}, u32[]{:S(2)}) copy-start(bf16[16,512]{1,0:T(8,128)(2,1)} %pv_hbm.1) | copy-start | bytes 49156
  2.1 1.2 %copy-start = (bf16[1,128,4096]{2,1,0:T(8,128)(2,1)S(1)}, bf16[1,128,4096]{2,1,0:T(8,128)(2,1)}, u32[]{:S(2)}) copy-start(bf16[1,128,4096]{2,1,0:T(8,128)(2,1)} %q_hbm.1) | copy-start | bytes 3145732
  3.4 1.2 %copy-start.1 = (bf16[1,128,4096]{2,1,0:T(8,128)(2,1)S(1)}, bf16[1,128,4096]{2,1,0:T(8,128)(2,1)}, u32[]{:S(2)}) copy-start(bf16[1,128,4096]{2,1,0:T(8,128)(2,1)} %do_hbm.1) | copy-start | bytes 3145732
  4.6 1.2 %copy-start.2 = (bf16[1,128,4096]{2,1,0:T(8,128)(2,1)S(1)}, bf16[1,128,4096]{2,1,0:T(8,128)(2,1)}, u32[]{:S(2)}) copy-start(bf16[1,128,4096]{2,1,0:T(8,128)(2,1)} %out_hbm.1) | copy-start | bytes 3145732
  5.8 0.9 %copy-start.3 = (bf16[1,128,512]{2,1,0:T(8,128)(2,1)S(1)}, bf16[1,128,512]{2,1,0:T(8,128)(2,1)}, u32[]{:S(2)}) copy-start(bf16[1,128,512]{2,1,0:T(8,128)(2,1)} %k_hbm.1) | copy-start | bytes 393220
  6.7 0.9 %copy-start.4 = (bf16[1,128,512]{2,1,0:T(8,128)(2,1)S(1)}, bf16[1,128,512]{2,1,0:T(8,128)(2,1)}, u32[]{:S(2)}) copy-start(bf16[1,128,512]{2,1,0:T(8,128)(2,1)} %v_hbm.1) | copy-start | bytes 393220

commit v2 on v1

v2 whole, which is shorter than its diff:
```python
import functools
import math

import jax
import jax.numpy as jnp
from jax import lax
from jax.experimental import pallas as pl
from jax.experimental.pallas import tpu as pltpu
from jax.sharding import PartitionSpec as P

H = 32
KVH = 4
HD = 128
G = H // KVH
MESH = pl.DeviceIdType.MESH
NT = (((1,), (1,)), ((), ()))
LOG2E = math.log2(math.e)
SCALE = HD ** (-0.5)
UB = 256


def dot(a, b):
    return jnp.dot(a, b, preferred_element_type=jnp.float32)


def dot_nt(a, b):
    return lax.dot_general(a, b, NT, preferred_element_type=jnp.float32)


def heads_to_rows(block):
    return jnp.concatenate([block[:, g * HD : (g + 1) * HD] for g in range(G)], 0)


def rows_to_lanes(block):
    return jnp.concatenate([block[g : g + 1] for g in range(G)], 1)


def part_grads(keys, values, queries, grads, lse_row, delta_row, live):
    scores = dot_nt(keys, queries)
    probs = jnp.exp2(scores * (SCALE * LOG2E) - lse_row)
    if live is not None:
        probs = jnp.where(live, probs, 0.0)
    prob_grad = dot_nt(values, grads)
    score_low = (probs * (prob_grad - delta_row)).astype(jnp.bfloat16)
    probs_low = probs.astype(jnp.bfloat16)
    dk = dot(score_low, queries) * SCALE
    dv = dot(probs_low, grads)
    return score_low, dk, dv


def kernel(
    n, ns, rows, length_hbm, q_hbm, k_hbm, v_hbm, do_hbm, out_hbm, lse_hbm, pk_hbm, pv_hbm,
    dq_hbm, dk_ref, dv_ref, pdk_ref, pdv_ref,
    length_ref, q_ref, k_ref, v_ref, do_ref, out_ref, lse_ref, dq_ref, lse_t, delta_t, score_grads,
    gathered, crossed, parts, landed, totals,
    load_sem, store_sem, gather_send, gather_recv, pass_send, pass_recv, cross_send, cross_recv,
    part_send, part_recv, total_send, total_recv,
):
    tokens = q_ref.shape[0]
    me = lax.axis_index("prefix")
    mine = lax.axis_index("sample")
    half = lax.rem(mine, 2)
    partner = {"sample": mine + 1 - 2 * half}
    heads = KVH // 2
    width = KVH * HD

    pairs = [
        (pk_hbm, gathered.at[0, 0]), (pv_hbm, gathered.at[1, 0]),
        (do_hbm.at[0], do_ref), (out_hbm.at[0], out_ref),
        (lse_hbm.at[0], lse_ref), (q_hbm.at[0], q_ref), (k_hbm.at[0], k_ref), (v_hbm.at[0], v_ref),
        (length_hbm, length_ref),
    ]
    loads = [pltpu.make_async_copy(a, b, load_sem.at[i]) for i, (a, b) in enumerate(pairs)]
    for copy in loads:
        copy.start()

    barrier = pltpu.get_barrier_semaphore()

    def greet(d, _):
        pl.semaphore_signal(
            barrier, inc=1, device_id={"prefix": lax.rem(me + d, n)}, device_id_type=MESH
        )
        return 0

    def greet_sample(d, _):
        pl.semaphore_signal(
            barrier, inc=1, device_id={"sample": lax.rem(mine + d, ns)}, device_id_type=MESH
        )
        return 0

    lax.fori_loop(1, n, greet, 0)
    lax.fori_loop(1, ns, greet_sample, 0)
    loads[0].wait()
    loads[1].wait()
    pl.semaphore_wait(barrier, n - 1 + ns - 1)

    def gather_copy(d):
        return pltpu.make_async_remote_copy(
            src_ref=gathered.at[half, 0],
            dst_ref=gathered.at[half, d],
            send_sem=gather_send.at[d],
            recv_sem=gather_recv.at[d],
            device_id={"prefix": lax.rem(me + d, n)},
            device_id_type=MESH,
        )

    def start_gather(d, _):
        gather_copy(d).start()
        return 0

    lax.fori_loop(1, n, start_gather, 0)

    for copy in loads[2:]:
        copy.wait()
    length = length_ref[0]
    key_pos = lax.broadcasted_iota(jnp.int32, (tokens, tokens), 0)
    query_pos = lax.broadcasted_iota(jnp.int32, (tokens, tokens), 1)
    causal = key_pos <= query_pos
    live_t = lax.broadcasted_iota(jnp.int32, (H, tokens), 1) < length
    lse_t[...] = jnp.where(live_t, lse_ref[...] * LOG2E, 1e30)
    prompt_rows = n * rows

    def own_step(j, _):
        cols = pl.ds(pl.multiple_of(j * G * HD, G * HD), G * HD)
        head = pl.ds(pl.multiple_of(j * HD, HD), HD)
        stat = pl.ds(pl.multiple_of(j * G, G), G)
        queries = heads_to_rows(q_ref[:, cols])
        grads = heads_to_rows(do_ref[:, cols])
        outs = heads_to_rows(out_ref[:, cols])
        product = grads.astype(jnp.float32) * outs.astype(jnp.float32)
        high = product.astype(jnp.bfloat16)
        low = (product - high.astype(jnp.float32)).astype(jnp.bfloat16)
        ones = jnp.ones((G, HD), jnp.bfloat16)
        sums = dot_nt(ones, high) + dot_nt(ones, low)
        delta_row = sums[0:1]
        for g in range(G):
            delta_t[j, g : g + 1, :] = delta_row[:, g * HD : (g + 1) * HD]
        lse_row = rows_to_lanes(lse_t[stat, :])
        live = jnp.concatenate([causal] * G, 1)
        score_low, dk, dv = part_grads(
            k_ref[:, head], v_ref[:, head], queries, grads, lse_row, delta_row, live
        )
        score_grads[j, prompt_rows:] = score_low
        dk_ref[0, :, head] = dk.astype(jnp.bfloat16)
        dv_ref[0, :, head] = dv.astype(jnp.bfloat16)
        return 0

    lax.fori_loop(0, KVH, own_step, 0)

    def pass_copy(d):
        return pltpu.make_async_remote_copy(
            src_ref=gathered.at[half, d],
            dst_ref=gathered.at[half, d],
            send_sem=pass_send.at[d],
            recv_sem=pass_recv.at[d],
            device_id=partner,
            device_id_type=MESH,
        )

    def pass_on(d, _):
        gather_copy(d).wait_recv()
        pass_copy(d).start()
        return 0

    def end_pass(d, _):
        pass_copy(d).wait_recv()
        return 0

    lax.fori_loop(1, n, pass_on, 0)
    lax.fori_loop(1, n, end_pass, 0)

    block = UB if prompt_rows % UB == 0 else prompt_rows

    def prompt_head(j, use):
        cols = pl.ds(pl.multiple_of(j * G * HD, G * HD), G * HD)
        head = pl.ds(pl.multiple_of(j * HD, HD), HD)
        stat = pl.ds(pl.multiple_of(j * G, G), G)
        queries = heads_to_rows(q_ref[:, cols])
        grads = heads_to_rows(do_ref[:, cols])
        lse_row = rows_to_lanes(lse_t[stat, :])
        delta_row = rows_to_lanes(delta_t[j])

        def block_step(b, _):
            at = pl.ds(pl.multiple_of(b * block, block), block)
            slots = pl.ds(b * (block // rows), block // rows)
            score_low, dk, dv = part_grads(
                gathered[0, slots, :, head].reshape(block, HD),
                gathered[1, slots, :, head].reshape(block, HD),
                queries, grads, lse_row, delta_row, None,
            )
            score_grads[j, at] = score_low
            use(slots, jnp.concatenate([dk, dv], 1).reshape(block // rows, rows, 2 * HD))
            return 0

        if prompt_rows == block:
            block_step(0, 0)
        else:
            lax.fori_loop(0, prompt_rows // block, block_step, 0)

    def cross_copy(i):
        return pltpu.make_async_remote_copy(
            src_ref=crossed.at[0, i],
            dst_ref=crossed.at[1, i],
            send_sem=cross_send.at[i],
            recv_sem=cross_recv.at[i],
            device_id=partner,
            device_id_type=MESH,
        )

    def cross_step(i, _):
        def use(slots, both):
            crossed[0, i, slots] = both

        prompt_head((1 - half) * heads + i, use)
        cross_copy(i).start()
        return 0

    lax.fori_loop(0, heads, cross_step, 0)

    def part_copy(i, d):
        return pltpu.make_async_remote_copy(
            src_ref=parts.at[i, d],
            dst_ref=landed.at[i, d],
            send_sem=part_send.at[i, d],
            recv_sem=part_recv.at[i, d],
            device_id={"prefix": lax.rem(me + n - d, n)},
            device_id_type=MESH,
        )

    def part_step(i, _):
        cross_copy(i).wait_recv()

        def use(slots, both):
            parts[i, slots] = (both + crossed[1, i, slots]).astype(jnp.bfloat16)

        prompt_head(half * heads + i, use)

        def start_part(d, _):
            part_copy(i, d).start()
            return 0

        lax.fori_loop(1, n, start_part, 0)
        return 0

    lax.fori_loop(0, heads, part_step, 0)

    def query_step(j, _):
        head = pl.ds(pl.multiple_of(j * HD, HD), HD)
        keys = jnp.concatenate(
            [gathered[0, :, :, head].reshape(prompt_rows, HD), k_ref[:, head]], 0
        )
        dq_t = (dot(keys.T, score_grads[j]) * SCALE).astype(jnp.bfloat16)
        for g in range(G):
            at = pl.ds(pl.multiple_of((j * G + g) * HD, HD), HD)
            dq_ref[:, at] = dq_t[:, g * HD : (g + 1) * HD].T
        return 0

    lax.fori_loop(0, KVH, query_step, 0)
    store = pltpu.make_async_copy(dq_ref, dq_hbm.at[0], store_sem)
    store.start()

    def end_sends(d, _):
        gather_copy(d).wait_send()
        pass_copy(d).wait_send()
        return 0

    lax.fori_loop(1, n, end_sends, 0)
    for i in range(heads):
        cross_copy(i).wait_send()

    def sum_step(i, _):
        def wait_part(d, _):
            part_copy(i, d).wait()
            return 0

        lax.fori_loop(1, n, wait_part, 0)
        others = jnp.sum(landed[i, 1:].astype(jnp.float32), 0)
        totals[mine, i] = others + parts[i, 0].astype(jnp.float32)
        return 0

    lax.fori_loop(0, heads, sum_step, 0)

    def total_copy(d):
        return pltpu.make_async_remote_copy(
            src_ref=totals.at[mine],
            dst_ref=totals.at[mine],
            send_sem=total_send.at[d],
            recv_sem=total_recv.at[d],
            device_id={"sample": lax.rem(mine + d, ns)},
            device_id_type=MESH,
        )

    for d in range(1, ns):
        total_copy(d).start()
    for d in range(1, ns):
        total_copy(d).wait()
    for j in range(KVH):
        both = totals[j // heads, j % heads]
        for s in range(2 + j // heads, ns, 2):
            both = both + totals[s, j % heads]
        pdk_ref[:, j * HD : (j + 1) * HD] = both[:, :HD]
        pdv_ref[:, j * HD : (j + 1) * HD] = both[:, HD:]
    store.wait()


def store_kernel(*refs):
    *arrays, sem = refs
    count = len(arrays) // 2
    copies = [
        pltpu.make_async_copy(arrays[i], arrays[count + i], sem.at[i]) for i in range(count)
    ]
    for copy in copies:
        copy.start()
    for copy in copies:
        copy.wait()


def body(resp_q, resp_k, resp_v, resp_do, resp_out, resp_lse, prompt_k, prompt_v, resp_lengths):
    n = lax.axis_size("prefix")
    ns = lax.axis_size("sample")
    rows, width = prompt_k.shape
    _, tokens, q_width = resp_q.shape
    bf16, f32 = jnp.bfloat16, jnp.float32
    heads = KVH // 2
    vmem = pl.BlockSpec(memory_space=pltpu.VMEM)
    hbm = pl.BlockSpec(memory_space=pltpu.HBM)
    free = pl.BlockSpec(memory_space=pl.ANY)
    dma = pltpu.SemaphoreType.DMA
    out_shape = (
        jax.ShapeDtypeStruct(resp_q.shape, bf16),
        jax.ShapeDtypeStruct(resp_k.shape, bf16),
        jax.ShapeDtypeStruct(resp_v.shape, bf16),
        jax.ShapeDtypeStruct((rows, width), f32),
        jax.ShapeDtypeStruct((rows, width), f32),
    )
    results = pl.pallas_call(
        functools.partial(kernel, n, ns, rows),
        out_shape=out_shape,
        in_specs=[hbm] * 9,
        out_specs=(free, vmem, vmem, vmem, vmem),
        scratch_shapes=[
            pltpu.SMEM((1,), jnp.int32),
            pltpu.VMEM((tokens, q_width), bf16),
            pltpu.VMEM((tokens, width), bf16),
            pltpu.VMEM((tokens, width), bf16),
            pltpu.VMEM((tokens, q_width), bf16),
            pltpu.VMEM((tokens, q_width), bf16),
            pltpu.VMEM((H, tokens), f32),
            pltpu.VMEM((tokens, q_width), bf16),
            pltpu.VMEM((H, tokens), f32),
            pltpu.VMEM((KVH, G, tokens), f32),
            pltpu.VMEM((KVH, n * rows + tokens, G * tokens), bf16),
            pltpu.VMEM((2, n, rows, width), bf16),
            pltpu.VMEM((2, heads, n, rows, 2 * HD), f32),
            pltpu.VMEM((heads, n, rows, 2 * HD), bf16),
            pltpu.VMEM((heads, n, rows, 2 * HD), bf16),
            pltpu.VMEM((ns, heads, rows, 2 * HD), f32),
            dma((9,)),
            dma(()),
            dma((n,)),
            dma((n,)),
            dma((n,)),
            dma((n,)),
            dma((heads,)),
            dma((heads,)),
            dma((heads, n)),
            dma((heads, n)),
            dma((ns,)),
            dma((ns,)),
        ],
        compiler_params=pltpu.CompilerParams(
            collective_id=0, has_side_effects=True, vmem_limit_bytes=63 * 1024 * 1024
        ),
        cost_estimate=pl.CostEstimate(
            flops=2_000_000_000, bytes_accessed=5_000_000, transcendentals=1_600_000
        ),
    )(
        resp_lengths, resp_q, resp_k, resp_v, resp_do, resp_out, jnp.swapaxes(resp_lse, 1, 2),
        prompt_k, prompt_v,
    )
    return pl.pallas_call(
        store_kernel,
        out_shape=out_shape,
        in_specs=[free] * 5,
        out_specs=(hbm,) * 5,
        scratch_shapes=[dma((5,))],
        compiler_params=pltpu.CompilerParams(vmem_limit_bytes=63 * 1024 * 1024),
    )(*results)


def solution(mesh):
    rows = P(("sample", "prefix"), None, None)
    prompt = P("prefix", None)
    return jax.shard_map(
        body,
        mesh=mesh,
        in_specs=(rows, rows, rows, rows, rows, rows, prompt, prompt, P(("sample", "prefix"))),
        out_specs=(rows, rows, rows, prompt, prompt),
        check_vma=False,
    )
```

time: 51.2 us -> 73.7 us (1.44)
  Pallas kernels: 39.7 us -> 72.2 us
  local copies, waits for them, and re-layouts: 9.82 us -> 0 us
    pallas_call x1 -> x2, Pallas kernels: 39.7 us -> 72.2 us  [the longest x1 42.8 us: body(): pl.pallas_call(store_kernel, out_shape=out_shape, in_specs=[free] * 5, ou...]
    unnamed x20 -> x0, local copies, waits for them, and re-layouts: 9.82 us -> none
where the time goes in v2:
time: 73.7 us; the launch traced here: 73.4 us
  Pallas kernels  72.2 us (98%)
  between operations  1.29 us (2%)
    pallas_call x1, Pallas kernels, body(): pl.pallas_call(store_kernel, out_shape=out_shape, in_specs=[free] * 5, ou...  42.8 us
    pallas_call x1, Pallas kernels, body(): pl.pallas_call(functools.partial(kernel, n, ns, rows), out_shape=out_shap...  29.3 us

profile of v2, /device:TPU:0, one launch (start us, length us, event | category | flops | bytes accessed | tf_op | source)
XLA Modules:
  0.0 73.4 jit_solution(7387642439145618589)
XLA Ops:
  1.3 29.3 %shard_map.128 = (bf16[1,128,4096]{2,1,0:T(8,128)(2,1)}, bf16[1,128,512]{2,1,0:T(8,128)(2,1)}, bf16[1,128,512]{2,1,0:T(8,128)(2,1)}, f32[16,512]{1,0:T(8,128)}, f32[16,512]{1,0:T(8,128)}) custom-call(s32[1]{0:T(128)S(6)} %copy.14.length_hbm, bf16[1,128,4096]{2,1,0:T(8,128)(2,1)} %q_hbm.1, bf16[1,128,512]{2,1,0:T(8,128)(2,1)} %k_hbm.1, ...), custom_call_target="tpu_custom_call" | custom-call | flops 2000000000 | bytes 5000000 | tf_op jit(solution)/shard_map/pallas_call | solution.py:336
  30.6 42.8 %shard_map.129 = (bf16[1,128,4096]{2,1,0:T(8,128)(2,1)}, bf16[1,128,512]{2,1,0:T(8,128)(2,1)}, bf16[1,128,512]{2,1,0:T(8,128)(2,1)}, f32[16,512]{1,0:T(8,128)}, f32[16,512]{1,0:T(8,128)}) custom-call(bf16[1,128,4096]{2,1,0:T(8,128)(2,1)} %get-tuple-element.10.refs_0_, bf16[1,128,512]{2,1,0:T(8,128)(2,1)} %get-tuple-element.11.refs_1_, ...), custom_call_target="tpu_custom_call" | custom-call | tf_op jit(solution)/shard_map/pallas_call | solution.py:381

commit v3 on v2

--- a/solution.py
+++ b/solution.py
@@ -27,31 +27,41 @@
     return lax.dot_general(a, b, NT, preferred_element_type=jnp.float32)
 
 
-def heads_to_rows(block):
-    return jnp.concatenate([block[:, g * HD : (g + 1) * HD] for g in range(G)], 0)
+def head_pair(ref, j):
+    def read(first):
+        at = [pl.ds(pl.multiple_of((j * G + g) * HD, HD), HD) for g in (first, first + 1)]
+        return jnp.concatenate([ref[:, cols] for cols in at], 0)
+
+    return read
 
 
 def rows_to_lanes(block):
     return jnp.concatenate([block[g : g + 1] for g in range(G)], 1)
 
 
-def part_grads(keys, values, queries, grads, lse_row, delta_row, live):
-    scores = dot_nt(keys, queries)
-    probs = jnp.exp2(scores * (SCALE * LOG2E) - lse_row)
-    if live is not None:
-        probs = jnp.where(live, probs, 0.0)
-    prob_grad = dot_nt(values, grads)
-    score_low = (probs * (prob_grad - delta_row)).astype(jnp.bfloat16)
-    probs_low = probs.astype(jnp.bfloat16)
-    dk = dot(score_low, queries) * SCALE
-    dv = dot(probs_low, grads)
-    return score_low, dk, dv
+def part_grads(keys, values, queries, grads, lse_row, delta_row, live, keep):
+    dk = dv = None
+    for first in range(0, G, 2):
+        chunk = slice(first * lse_row.shape[1] // G, (first + 2) * lse_row.shape[1] // G)
+        query, grad = queries(first), grads(first)
+        scores = dot_nt(keys, query)
+        probs = jnp.exp2(scores * (SCALE * LOG2E) - lse_row[:, chunk])
+        if live is not None:
+            probs = jnp.where(live, probs, 0.0)
+        prob_grad = dot_nt(values, grad)
+        score_low = (probs * (prob_grad - delta_row[:, chunk])).astype(jnp.bfloat16)
+        keep(chunk, score_low)
+        dk_term = dot(score_low, query)
+        dv_term = dot(probs.astype(jnp.bfloat16), grad)
+        dk = dk_term if dk is None else dk + dk_term
+        dv = dv_term if dv is None else dv + dv_term
+    return dk * SCALE, dv
 
 
 def kernel(
     n, ns, rows, length_hbm, q_hbm, k_hbm, v_hbm, do_hbm, out_hbm, lse_hbm, pk_hbm, pv_hbm,
-    dq_hbm, dk_ref, dv_ref, pdk_ref, pdv_ref,
-    length_ref, q_ref, k_ref, v_ref, do_ref, out_ref, lse_ref, dq_ref, lse_t, delta_t, score_grads,
+    dq_hbm, dk_hbm, dv_hbm, pdk_ref, pdv_ref,
+    dk_ref, dv_ref, length_ref, q_ref, k_ref, v_ref, do_ref, out_ref, lse_ref, dq_ref, lse_t, delta_t, score_grads,
     gathered, crossed, parts, landed, totals,
     load_sem, store_sem, gather_send, gather_recv, pass_send, pass_recv, cross_send, cross_recv,
     part_send, part_recv, total_send, total_recv,
@@ -71,8 +81,8 @@
         (length_hbm, length_ref),
     ]
     loads = [pltpu.make_async_copy(a, b, load_sem.at[i]) for i, (a, b) in enumerate(pairs)]
-    for copy in loads:
-        copy.start()
+    loads[0].start()
+    loads[1].start()
 
     barrier = pltpu.get_barrier_semaphore()
 
@@ -90,6 +100,8 @@
 
     lax.fori_loop(1, n, greet, 0)
     lax.fori_loop(1, ns, greet_sample, 0)
+    for copy in loads[2:]:
+        copy.start()
     loads[0].wait()
     loads[1].wait()
     pl.semaphore_wait(barrier, n - 1 + ns - 1)
@@ -121,31 +133,39 @@
     prompt_rows = n * rows
 
     def own_step(j, _):
-        cols = pl.ds(pl.multiple_of(j * G * HD, G * HD), G * HD)
         head = pl.ds(pl.multiple_of(j * HD, HD), HD)
         stat = pl.ds(pl.multiple_of(j * G, G), G)
-        queries = heads_to_rows(q_ref[:, cols])
-        grads = heads_to_rows(do_ref[:, cols])
-        outs = heads_to_rows(out_ref[:, cols])
-        product = grads.astype(jnp.float32) * outs.astype(jnp.float32)
-        high = product.astype(jnp.bfloat16)
-        low = (product - high.astype(jnp.float32)).astype(jnp.bfloat16)
         ones = jnp.ones((G, HD), jnp.bfloat16)
-        sums = dot_nt(ones, high) + dot_nt(ones, low)
-        delta_row = sums[0:1]
-        for g in range(G):
-            delta_t[j, g : g + 1, :] = delta_row[:, g * HD : (g + 1) * HD]
+        sums = []
+        for first in range(0, G, 2):
+            grads = head_pair(do_ref, j)(first).astype(jnp.float32)
+            product = grads * head_pair(out_ref, j)(first).astype(jnp.float32)
+            high = product.astype(jnp.bfloat16)
+            low = (product - high.astype(jnp.float32)).astype(jnp.bfloat16)
+            sums.append((dot_nt(ones, high) + dot_nt(ones, low))[0:1])
+        delta_row = jnp.concatenate(sums, 1)
+        delta_t[j] = delta_row
         lse_row = rows_to_lanes(lse_t[stat, :])
-        live = jnp.concatenate([causal] * G, 1)
-        score_low, dk, dv = part_grads(
-            k_ref[:, head], v_ref[:, head], queries, grads, lse_row, delta_row, live
-        )
-        score_grads[j, prompt_rows:] = score_low
-        dk_ref[0, :, head] = dk.astype(jnp.bfloat16)
-        dv_ref[0, :, head] = dv.astype(jnp.bfloat16)
+
+        def keep(chunk, score_low):
+            score_grads[j, prompt_rows:, chunk] = score_low
+
+        dk, dv = part_grads(
+            k_ref[:, head], v_ref[:, head], head_pair(q_ref, j), head_pair(do_ref, j),
+            lse_row, delta_row, jnp.concatenate([causal] * 2, 1), keep,
+        )
+        dk_ref[:, head] = dk.astype(jnp.bfloat16)
+        dv_ref[:, head] = dv.astype(jnp.bfloat16)
         return 0
 
     lax.fori_loop(0, KVH, own_step, 0)
+    stores = [
+        pltpu.make_async_copy(dk_ref, dk_hbm.at[0], store_sem.at[0]),
+        pltpu.make_async_copy(dv_ref, dv_hbm.at[0], store_sem.at[1]),
+        pltpu.make_async_copy(dq_ref, dq_hbm.at[0], store_sem.at[2]),
+    ]
+    stores[0].start()
+    stores[1].start()
 
     def pass_copy(d):
         return pltpu.make_async_remote_copy(
@@ -172,23 +192,23 @@
     block = UB if prompt_rows % UB == 0 else prompt_rows
 
     def prompt_head(j, use):
-        cols = pl.ds(pl.multiple_of(j * G * HD, G * HD), G * HD)
         head = pl.ds(pl.multiple_of(j * HD, HD), HD)
         stat = pl.ds(pl.multiple_of(j * G, G), G)
-        queries = heads_to_rows(q_ref[:, cols])
-        grads = heads_to_rows(do_ref[:, cols])
         lse_row = rows_to_lanes(lse_t[stat, :])
-        delta_row = rows_to_lanes(delta_t[j])
+        delta_row = delta_t[j]
 
         def block_step(b, _):
             at = pl.ds(pl.multiple_of(b * block, block), block)
             slots = pl.ds(b * (block // rows), block // rows)
-            score_low, dk, dv = part_grads(
+
+            def keep(chunk, score_low):
+                score_grads[j, at, chunk] = score_low
+
+            dk, dv = part_grads(
                 gathered[0, slots, :, head].reshape(block, HD),
                 gathered[1, slots, :, head].reshape(block, HD),
-                queries, grads, lse_row, delta_row, None,
+                head_pair(q_ref, j), head_pair(do_ref, j), lse_row, delta_row, None, keep,
             )
-            score_grads[j, at] = score_low
             use(slots, jnp.concatenate([dk, dv], 1).reshape(block // rows, rows, 2 * HD))
             return 0
 
@@ -256,8 +276,7 @@
         return 0
 
     lax.fori_loop(0, KVH, query_step, 0)
-    store = pltpu.make_async_copy(dq_ref, dq_hbm.at[0], store_sem)
-    store.start()
+    stores[2].start()
 
     def end_sends(d, _):
         gather_copy(d).wait_send()
@@ -300,7 +319,8 @@
             both = both + totals[s, j % heads]
         pdk_ref[:, j * HD : (j + 1) * HD] = both[:, :HD]
         pdv_ref[:, j * HD : (j + 1) * HD] = both[:, HD:]
-    store.wait()
+    for store in stores:
+        store.wait()
 
 
 def store_kernel(*refs):
@@ -333,12 +353,19 @@
         jax.ShapeDtypeStruct((rows, width), f32),
         jax.ShapeDtypeStruct((rows, width), f32),
     )
+    args = (
+        resp_lengths, resp_q, resp_k, resp_v, resp_do, resp_out, jnp.swapaxes(resp_lse, 1, 2),
+        prompt_k, prompt_v,
+    )
+    args = args[:1] + tuple(pltpu.with_memory_space_constraint(arg, pltpu.HBM) for arg in args[1:])
     results = pl.pallas_call(
         functools.partial(kernel, n, ns, rows),
-        out_shape=out_shape,
+        out_shape=tuple(pltpu.VMEM(o.shape, o.dtype) for o in out_shape),
         in_specs=[hbm] * 9,
-        out_specs=(free, vmem, vmem, vmem, vmem),
+        out_specs=(free, free, free, vmem, vmem),
         scratch_shapes=[
+            pltpu.VMEM((tokens, width), bf16),
+            pltpu.VMEM((tokens, width), bf16),
             pltpu.SMEM((1,), jnp.int32),
             pltpu.VMEM((tokens, q_width), bf16),
             pltpu.VMEM((tokens, width), bf16),
@@ -348,7 +375,7 @@
             pltpu.VMEM((H, tokens), f32),
             pltpu.VMEM((tokens, q_width), bf16),
             pltpu.VMEM((H, tokens), f32),
-            pltpu.VMEM((KVH, G, tokens), f32),
+            pltpu.VMEM((KVH, 1, G * tokens), f32),
             pltpu.VMEM((KVH, n * rows + tokens, G * tokens), bf16),
             pltpu.VMEM((2, n, rows, width), bf16),
             pltpu.VMEM((2, heads, n, rows, 2 * HD), f32),
@@ -356,7 +383,7 @@
             pltpu.VMEM((heads, n, rows, 2 * HD), bf16),
             pltpu.VMEM((ns, heads, rows, 2 * HD), f32),
             dma((9,)),
-            dma(()),
+            dma((3,)),
             dma((n,)),
             dma((n,)),
             dma((n,)),
@@ -369,22 +396,18 @@
             dma((ns,)),
         ],
         compiler_params=pltpu.CompilerParams(
-            collective_id=0, has_side_effects=True, vmem_limit_bytes=63 * 1024 * 1024
+            collective_id=0, has_side_effects=True, vmem_limit_bytes=48 * 1024 * 1024
         ),
         cost_estimate=pl.CostEstimate(
             flops=2_000_000_000, bytes_accessed=5_000_000, transcendentals=1_600_000
         ),
-    )(
-        resp_lengths, resp_q, resp_k, resp_v, resp_do, resp_out, jnp.swapaxes(resp_lse, 1, 2),
-        prompt_k, prompt_v,
-    )
+    )(*args)
     return pl.pallas_call(
         store_kernel,
         out_shape=out_shape,
         in_specs=[free] * 5,
         out_specs=(hbm,) * 5,
         scratch_shapes=[dma((5,))],
-        compiler_params=pltpu.CompilerParams(vmem_limit_bytes=63 * 1024 * 1024),
     )(*results)
 
 

time: 73.7 us -> 77.2 us (1.047)
  local copies, waits for them, and re-layouts: 0 us -> 3.45 us
    unnamed x0 -> x10, local copies, waits for them, and re-layouts: none -> 3.45 us
where the time goes in v3:
time: 77.2 us; the launch traced here: 76.9 us
  Pallas kernels  72.2 us (94%)
  local copies, waits for them, and re-layouts  3.45 us (4%)
  between operations  1.3 us (2%)
    pallas_call x1, Pallas kernels, body(): pl.pallas_call(store_kernel, out_shape=out_shape, in_specs=[free] * 5, ou...  42.8 us
    pallas_call x1, Pallas kernels, body(): pl.pallas_call(functools.partial(kernel, n, ns, rows), out_shape=tuple((p...  29.4 us
    unnamed x10, local copies, waits for them, and re-layouts  3.45 us

profile of v3, /device:TPU:0, one launch (start us, length us, event | category | flops | bytes accessed | tf_op | source)
XLA Modules:
  0.0 76.9 jit_solution(16942157191678236011)
XLA Ops:
  1.3 29.4 %shard_map.128 = (bf16[1,128,4096]{2,1,0:T(8,128)(2,1)S(1)}, bf16[1,128,512]{2,1,0:T(8,128)(2,1)S(1)}, bf16[1,128,512]{2,1,0:T(8,128)(2,1)S(1)}, f32[16,512]{1,0:T(8,128)S(1)}, f32[16,512]{1,0:T(8,128)S(1)}) custom-call(s32[1]{0:T(128)S(6)} %copy.14.length_hbm, bf16[1,128,4096]{2,1,0:T(8,128)(2,1)} %q_hbm.1, bf16[1,128,512]{2,1,0:T(8,128)(2,1)} %k_hbm.1, ...), custom_call_target="tpu_custom_call" | custom-call | flops 2000000000 | bytes 5000000 | tf_op jit(solution)/shard_map/pallas_call | solution.py:361
  30.6 0.0 copy-start
  30.7 1.0 %copy-done = bf16[1,128,4096]{2,1,0:T(8,128)(2,1)} copy-done((bf16[1,128,4096]{2,1,0:T(8,128)(2,1)}, bf16[1,128,4096]{2,1,0:T(8,128)(2,1)S(1)}, u32[]{:S(2)}) %copy-start) | copy-done | bytes 1048600
  31.6 0.0 copy-start.1
  31.6 0.6 copy-done.1
  32.3 0.0 copy-start.2
  32.3 0.6 copy-done.2
  32.9 0.0 copy-start.3
  32.9 0.6 copy-done.3
  33.5 0.0 copy-start.4
  33.5 0.6 copy-done.4
  34.1 42.8 %shard_map.129 = (bf16[1,128,4096]{2,1,0:T(8,128)(2,1)}, bf16[1,128,512]{2,1,0:T(8,128)(2,1)}, bf16[1,128,512]{2,1,0:T(8,128)(2,1)}, f32[16,512]{1,0:T(8,128)}, f32[16,512]{1,0:T(8,128)}) custom-call(bf16[1,128,4096]{2,1,0:T(8,128)(2,1)} %copy-done, bf16[1,128,512]{2,1,0:T(8,128)(2,1)} %copy-done.1, bf16[1,128,512]{2,1,0:T(8,128)(2,1)} %copy-done.2, ...), custom_call_target="tpu_custom_call" | custom-call | tf_op jit(solution)/shard_map/pallas_call | solution.py:405
Async XLA Ops:
  30.6 1.0 %copy-start = (bf16[1,128,4096]{2,1,0:T(8,128)(2,1)}, bf16[1,128,4096]{2,1,0:T(8,128)(2,1)S(1)}, u32[]{:S(2)}) copy-start(bf16[1,128,4096]{2,1,0:T(8,128)(2,1)S(1)} %get-tuple-element.10.refs_0_) | copy-start | bytes 3145732
  31.6 0.6 copy-start.1
  32.3 0.6 copy-start.2
  32.9 0.6 copy-start.3
  33.5 0.6 copy-start.4

commit v4 on v3

--- a/solution.py
+++ b/solution.py
@@ -81,8 +81,6 @@
         (length_hbm, length_ref),
     ]
     loads = [pltpu.make_async_copy(a, b, load_sem.at[i]) for i, (a, b) in enumerate(pairs)]
-    loads[0].start()
-    loads[1].start()
 
     barrier = pltpu.get_barrier_semaphore()
 
@@ -100,15 +98,13 @@
 
     lax.fori_loop(1, n, greet, 0)
     lax.fori_loop(1, ns, greet_sample, 0)
-    for copy in loads[2:]:
+    for copy in loads:
         copy.start()
-    loads[0].wait()
-    loads[1].wait()
     pl.semaphore_wait(barrier, n - 1 + ns - 1)
 
-    def gather_copy(d):
+    def gather_copy(d, source=pk_hbm):
         return pltpu.make_async_remote_copy(
-            src_ref=gathered.at[half, 0],
+            src_ref=source,
             dst_ref=gathered.at[half, d],
             send_sem=gather_send.at[d],
             recv_sem=gather_recv.at[d],
@@ -116,13 +112,17 @@
             device_id_type=MESH,
         )
 
-    def start_gather(d, _):
-        gather_copy(d).start()
-        return 0
-
-    lax.fori_loop(1, n, start_gather, 0)
-
-    for copy in loads[2:]:
+    for which, source in enumerate((pk_hbm, pv_hbm)):
+
+        @pl.when(half == which)
+        def _():
+            def start_gather(d, _):
+                gather_copy(d, source).start()
+                return 0
+
+            lax.fori_loop(1, n, start_gather, 0)
+
+    for copy in loads:
         copy.wait()
     length = length_ref[0]
     key_pos = lax.broadcasted_iota(jnp.int32, (tokens, tokens), 0)
@@ -130,21 +130,19 @@
     causal = key_pos <= query_pos
     live_t = lax.broadcasted_iota(jnp.int32, (H, tokens), 1) < length
     lse_t[...] = jnp.where(live_t, lse_ref[...] * LOG2E, 1e30)
+    lanes = lax.broadcasted_iota(jnp.int32, (tokens, HD), 1)
+    deltas = jnp.zeros((tokens, HD), jnp.float32)
+    for h in range(H):
+        at = slice(h * HD, (h + 1) * HD)
+        product = do_ref[:, at].astype(jnp.float32) * out_ref[:, at].astype(jnp.float32)
+        deltas = jnp.where(lanes == h, jnp.sum(product, 1, keepdims=True), deltas)
+    delta_t[...] = deltas.T
     prompt_rows = n * rows
 
     def own_step(j, _):
         head = pl.ds(pl.multiple_of(j * HD, HD), HD)
         stat = pl.ds(pl.multiple_of(j * G, G), G)
-        ones = jnp.ones((G, HD), jnp.bfloat16)
-        sums = []
-        for first in range(0, G, 2):
-            grads = head_pair(do_ref, j)(first).astype(jnp.float32)
-            product = grads * head_pair(out_ref, j)(first).astype(jnp.float32)
-            high = product.astype(jnp.bfloat16)
-            low = (product - high.astype(jnp.float32)).astype(jnp.bfloat16)
-            sums.append((dot_nt(ones, high) + dot_nt(ones, low))[0:1])
-        delta_row = jnp.concatenate(sums, 1)
-        delta_t[j] = delta_row
+        delta_row = rows_to_lanes(delta_t[stat, :])
         lse_row = rows_to_lanes(lse_t[stat, :])
 
         def keep(chunk, score_low):
@@ -195,7 +193,7 @@
         head = pl.ds(pl.multiple_of(j * HD, HD), HD)
         stat = pl.ds(pl.multiple_of(j * G, G), G)
         lse_row = rows_to_lanes(lse_t[stat, :])
-        delta_row = delta_t[j]
+        delta_row = rows_to_lanes(delta_t[stat, :])
 
         def block_step(b, _):
             at = pl.ds(pl.multiple_of(b * block, block), block)
@@ -375,7 +373,7 @@
             pltpu.VMEM((H, tokens), f32),
             pltpu.VMEM((tokens, q_width), bf16),
             pltpu.VMEM((H, tokens), f32),
-            pltpu.VMEM((KVH, 1, G * tokens), f32),
+            pltpu.VMEM((HD, tokens), f32),
             pltpu.VMEM((KVH, n * rows + tokens, G * tokens), bf16),
             pltpu.VMEM((2, n, rows, width), bf16),
             pltpu.VMEM((2, heads, n, rows, 2 * HD), f32),
@@ -405,10 +403,11 @@
     return pl.pallas_call(
         store_kernel,
         out_shape=out_shape,
-        in_specs=[free] * 5,
+        in_specs=[vmem] * 5,
         out_specs=(hbm,) * 5,
         scratch_shapes=[dma((5,))],
-    )(*results)
+        compiler_params=pltpu.CompilerParams(vmem_limit_bytes=4 * 1024 * 1024),
+    )(*(pltpu.with_memory_space_constraint(array, pltpu.VMEM) for array in results))
 
 
 def solution(mesh):

time: 77.2 us -> 32.3 us (0.42)
  Pallas kernels: 72.2 us -> 30.8 us
  local copies, waits for them, and re-layouts: 3.45 us -> 0 us
    pallas_call x1, Pallas kernels: 42.8 us -> 1.1 us  [body(): pl.pallas_call(store_kernel, out_shape=out_shape, in_specs=[vmem] * 5, ou...]
    unnamed x10 -> x0, local copies, waits for them, and re-layouts: 3.45 us -> none
where the time goes in v4:
time: 32.3 us; the launch traced here: 32.1 us
  Pallas kernels  30.8 us (95%)
  between operations  1.29 us (4%)
    pallas_call x1, Pallas kernels, body(): pl.pallas_call(functools.partial(kernel, n, ns, rows), out_shape=tuple((p...  29.7 us
    pallas_call x1, Pallas kernels, body(): pl.pallas_call(store_kernel, out_shape=out_shape, in_specs=[vmem] * 5, ou...  1.1 us

profile of v4, /device:TPU:0, one launch (start us, length us, event | category | flops | bytes accessed | tf_op | source)
XLA Modules:
  0.0 32.1 jit_solution(13299364566910763567)
XLA Ops:
  1.3 29.7 %shard_map.128 = (bf16[1,128,4096]{2,1,0:T(8,128)(2,1)S(1)}, bf16[1,128,512]{2,1,0:T(8,128)(2,1)S(1)}, bf16[1,128,512]{2,1,0:T(8,128)(2,1)S(1)}, f32[16,512]{1,0:T(8,128)S(1)}, f32[16,512]{1,0:T(8,128)S(1)}) custom-call(s32[1]{0:T(128)S(6)} %copy.14.length_hbm, bf16[1,128,4096]{2,1,0:T(8,128)(2,1)} %q_hbm.1, bf16[1,128,512]{2,1,0:T(8,128)(2,1)} %k_hbm.1, ...), custom_call_target="tpu_custom_call" | custom-call | flops 2000000000 | bytes 5000000 | tf_op jit(solution)/shard_map/pallas_call | solution.py:359
  31.0 1.1 %shard_map.129 = (bf16[1,128,4096]{2,1,0:T(8,128)(2,1)}, bf16[1,128,512]{2,1,0:T(8,128)(2,1)}, bf16[1,128,512]{2,1,0:T(8,128)(2,1)}, f32[16,512]{1,0:T(8,128)}, f32[16,512]{1,0:T(8,128)}) custom-call(bf16[1,128,4096]{2,1,0:T(8,128)(2,1)S(1)} %get-tuple-element.10.refs_0_, bf16[1,128,512]{2,1,0:T(8,128)(2,1)S(1)} %get-tuple-element.11.refs_1_, ...), custom_call_target="tpu_custom_call" | custom-call | tf_op jit(solution)/shard_map/pallas_call | solution.py:403

commit v5 on v4

--- a/solution.py
+++ b/solution.py
@@ -40,19 +40,26 @@
 
 
 def part_grads(keys, values, queries, grads, lse_row, delta_row, live, keep):
+    tokens = lse_row.shape[1] // G
     dk = dv = None
+
+    def products(first):
+        query, grad = queries(first), grads(first)
+        return query, grad, dot_nt(keys, query), dot_nt(values, grad)
+
+    ahead = products(0)
     for first in range(0, G, 2):
-        chunk = slice(first * lse_row.shape[1] // G, (first + 2) * lse_row.shape[1] // G)
-        query, grad = queries(first), grads(first)
-        scores = dot_nt(keys, query)
+        query, grad, scores, prob_grad = ahead
+        if first + 2 < G:
+            ahead = products(first + 2)
+        chunk = slice(first * tokens, (first + 2) * tokens)
         probs = jnp.exp2(scores * (SCALE * LOG2E) - lse_row[:, chunk])
         if live is not None:
             probs = jnp.where(live, probs, 0.0)
-        prob_grad = dot_nt(values, grad)
+        dv_term = dot(probs.astype(jnp.bfloat16), grad)
         score_low = (probs * (prob_grad - delta_row[:, chunk])).astype(jnp.bfloat16)
         keep(chunk, score_low)
         dk_term = dot(score_low, query)
-        dv_term = dot(probs.astype(jnp.bfloat16), grad)
         dk = dk_term if dk is None else dk + dk_term
         dv = dv_term if dv is None else dv + dv_term
     return dk * SCALE, dv
@@ -233,7 +240,8 @@
         cross_copy(i).start()
         return 0
 
-    lax.fori_loop(0, heads, cross_step, 0)
+    for i in range(heads):
+        cross_step(i, 0)
 
     def part_copy(i, d):
         return pltpu.make_async_remote_copy(
@@ -260,7 +268,8 @@
         lax.fori_loop(1, n, start_part, 0)
         return 0
 
-    lax.fori_loop(0, heads, part_step, 0)
+    for i in range(heads):
+        part_step(i, 0)
 
     def query_step(j, _):
         head = pl.ds(pl.multiple_of(j * HD, HD), HD)

time: 32.3 us -> 31.5 us (0.975)
  Pallas kernels: 30.8 us -> 30.1 us
    pallas_call x1, Pallas kernels: 29.7 us -> 28.9 us  [body(): pl.pallas_call(functools.partial(kernel, n, ns, rows), out_shape=tuple((p...]
where the time goes in v5:
time: 31.5 us; the launch traced here: 31.3 us
  Pallas kernels  30.1 us (96%)
  between operations  1.29 us (4%)
    pallas_call x1, Pallas kernels, body(): pl.pallas_call(functools.partial(kernel, n, ns, rows), out_shape=tuple((p...  28.9 us
    pallas_call x1, Pallas kernels, body(): pl.pallas_call(store_kernel, out_shape=out_shape, in_specs=[vmem] * 5, ou...  1.1 us

profile of v5, /device:TPU:0, one launch (start us, length us, event | category | flops | bytes accessed | tf_op | source)
XLA Modules:
  0.0 31.3 jit_solution(11821328634619753515)
XLA Ops:
  1.3 28.9 %shard_map.128 = (bf16[1,128,4096]{2,1,0:T(8,128)(2,1)S(1)}, bf16[1,128,512]{2,1,0:T(8,128)(2,1)S(1)}, bf16[1,128,512]{2,1,0:T(8,128)(2,1)S(1)}, f32[16,512]{1,0:T(8,128)S(1)}, f32[16,512]{1,0:T(8,128)S(1)}) custom-call(s32[1]{0:T(128)S(6)} %copy.14.length_hbm, bf16[1,128,4096]{2,1,0:T(8,128)(2,1)} %q_hbm.1, bf16[1,128,512]{2,1,0:T(8,128)(2,1)} %k_hbm.1, ...), custom_call_target="tpu_custom_call" | custom-call | flops 2000000000 | bytes 5000000 | tf_op jit(solution)/shard_map/pallas_call | solution.py:368
  30.2 1.1 %shard_map.129 = (bf16[1,128,4096]{2,1,0:T(8,128)(2,1)}, bf16[1,128,512]{2,1,0:T(8,128)(2,1)}, bf16[1,128,512]{2,1,0:T(8,128)(2,1)}, f32[16,512]{1,0:T(8,128)}, f32[16,512]{1,0:T(8,128)}) custom-call(bf16[1,128,4096]{2,1,0:T(8,128)(2,1)S(1)} %get-tuple-element.10.refs_0_, bf16[1,128,512]{2,1,0:T(8,128)(2,1)S(1)} %get-tuple-element.11.refs_1_, ...), custom_call_target="tpu_custom_call" | custom-call | tf_op jit(solution)/shard_map/pallas_call | solution.py:412

commit v6 on v5

--- a/solution.py
+++ b/solution.py
@@ -68,9 +68,10 @@
 def kernel(
     n, ns, rows, length_hbm, q_hbm, k_hbm, v_hbm, do_hbm, out_hbm, lse_hbm, pk_hbm, pv_hbm,
     dq_hbm, dk_hbm, dv_hbm, pdk_ref, pdv_ref,
-    dk_ref, dv_ref, length_ref, q_ref, k_ref, v_ref, do_ref, out_ref, lse_ref, dq_ref, lse_t, delta_t, score_grads,
-    gathered, crossed, parts, landed, totals,
-    load_sem, store_sem, gather_send, gather_recv, pass_send, pass_recv, cross_send, cross_recv,
+    dk_ref, dv_ref, length_ref, q_ref, k_ref, v_ref, do_ref, out_ref, lse_ref, dq_ref,
+    stats, own_low, prompt_low, q_other, do_other, stats_other, dq_other,
+    gathered, parts, landed, totals,
+    load_sem, store_sem, gather_send, gather_recv, swap_send, swap_recv, back_send, back_recv,
     part_send, part_recv, total_send, total_recv,
 ):
     tokens = q_ref.shape[0]
@@ -79,15 +80,22 @@
     half = lax.rem(mine, 2)
     partner = {"sample": mine + 1 - 2 * half}
     heads = KVH // 2
-    width = KVH * HD
-
+    prompt_rows = n * rows
+
+    def half_cols(which, size):
+        return pl.ds(pl.multiple_of(which * size, size), size)
+
+    prompt_cols = half_cols(half, heads * HD)
     pairs = [
-        (pk_hbm, gathered.at[0, 0]), (pv_hbm, gathered.at[1, 0]),
+        (pk_hbm.at[:, prompt_cols], gathered.at[0, 0]),
+        (pv_hbm.at[:, prompt_cols], gathered.at[0, 1]),
         (do_hbm.at[0], do_ref), (out_hbm.at[0], out_ref),
         (lse_hbm.at[0], lse_ref), (q_hbm.at[0], q_ref), (k_hbm.at[0], k_ref), (v_hbm.at[0], v_ref),
         (length_hbm, length_ref),
     ]
     loads = [pltpu.make_async_copy(a, b, load_sem.at[i]) for i, (a, b) in enumerate(pairs)]
+    loads[0].start()
+    loads[1].start()
 
     barrier = pltpu.get_barrier_semaphore()
 
@@ -105,55 +113,71 @@
 
     lax.fori_loop(1, n, greet, 0)
     lax.fori_loop(1, ns, greet_sample, 0)
-    for copy in loads:
+    for copy in loads[2:]:
         copy.start()
+    loads[0].wait()
+    loads[1].wait()
     pl.semaphore_wait(barrier, n - 1 + ns - 1)
 
-    def gather_copy(d, source=pk_hbm):
+    def gather_copy(d):
         return pltpu.make_async_remote_copy(
-            src_ref=source,
-            dst_ref=gathered.at[half, d],
+            src_ref=gathered.at[0],
+            dst_ref=gathered.at[d],
             send_sem=gather_send.at[d],
             recv_sem=gather_recv.at[d],
             device_id={"prefix": lax.rem(me + d, n)},
             device_id_type=MESH,
         )
 
-    for which, source in enumerate((pk_hbm, pv_hbm)):
-
-        @pl.when(half == which)
-        def _():
-            def start_gather(d, _):
-                gather_copy(d, source).start()
-                return 0
-
-            lax.fori_loop(1, n, start_gather, 0)
-
-    for copy in loads:
+    def start_gather(d, _):
+        gather_copy(d).start()
+        return 0
+
+    lax.fori_loop(1, n, start_gather, 0)
+
+    def swap_copy(i, source, target):
+        return pltpu.make_async_remote_copy(
+            src_ref=source,
+            dst_ref=target,
+            send_sem=swap_send.at[i],
+            recv_sem=swap_recv.at[i],
+            device_id=partner,
+            device_id_type=MESH,
+        )
+
+    query_cols = half_cols(1 - half, heads * G * HD)
+    swaps = [
+        swap_copy(0, q_hbm.at[0, :, query_cols], q_other),
+        swap_copy(1, do_hbm.at[0, :, query_cols], do_other),
+        swap_copy(2, stats.at[:, half_cols(1 - half, heads * G)], stats_other),
+    ]
+    swaps[0].start()
+    swaps[1].start()
+    for copy in loads[2:]:
         copy.wait()
     length = length_ref[0]
     key_pos = lax.broadcasted_iota(jnp.int32, (tokens, tokens), 0)
     query_pos = lax.broadcasted_iota(jnp.int32, (tokens, tokens), 1)
     causal = key_pos <= query_pos
     live_t = lax.broadcasted_iota(jnp.int32, (H, tokens), 1) < length
-    lse_t[...] = jnp.where(live_t, lse_ref[...] * LOG2E, 1e30)
+    stats[0] = jnp.where(live_t, lse_ref[...] * LOG2E, 1e30)
     lanes = lax.broadcasted_iota(jnp.int32, (tokens, HD), 1)
     deltas = jnp.zeros((tokens, HD), jnp.float32)
     for h in range(H):
         at = slice(h * HD, (h + 1) * HD)
         product = do_ref[:, at].astype(jnp.float32) * out_ref[:, at].astype(jnp.float32)
         deltas = jnp.where(lanes == h, jnp.sum(product, 1, keepdims=True), deltas)
-    delta_t[...] = deltas.T
-    prompt_rows = n * rows
+    stats[1] = deltas.T[:H]
+    swaps[2].start()
 
     def own_step(j, _):
         head = pl.ds(pl.multiple_of(j * HD, HD), HD)
         stat = pl.ds(pl.multiple_of(j * G, G), G)
-        delta_row = rows_to_lanes(delta_t[stat, :])
-        lse_row = rows_to_lanes(lse_t[stat, :])
+        lse_row = rows_to_lanes(stats[0, stat, :])
+        delta_row = rows_to_lanes(stats[1, stat, :])
 
         def keep(chunk, score_low):
-            score_grads[j, prompt_rows:, chunk] = score_low
+            own_low[j, :, chunk] = score_low
 
         dk, dv = part_grads(
             k_ref[:, head], v_ref[:, head], head_pair(q_ref, j), head_pair(do_ref, j),
@@ -172,76 +196,15 @@
     stores[0].start()
     stores[1].start()
 
-    def pass_copy(d):
-        return pltpu.make_async_remote_copy(
-            src_ref=gathered.at[half, d],
-            dst_ref=gathered.at[half, d],
-            send_sem=pass_send.at[d],
-            recv_sem=pass_recv.at[d],
-            device_id=partner,
-            device_id_type=MESH,
-        )
-
-    def pass_on(d, _):
-        gather_copy(d).wait_recv()
-        pass_copy(d).start()
-        return 0
-
-    def end_pass(d, _):
-        pass_copy(d).wait_recv()
-        return 0
-
-    lax.fori_loop(1, n, pass_on, 0)
-    lax.fori_loop(1, n, end_pass, 0)
+    def end_gather(d, _):
+        gather_copy(d).wait()
+        return 0
+
+    lax.fori_loop(1, n, end_gather, 0)
+    for copy in swaps:
+        copy.wait()
 
     block = UB if prompt_rows % UB == 0 else prompt_rows
-
-    def prompt_head(j, use):
-        head = pl.ds(pl.multiple_of(j * HD, HD), HD)
-        stat = pl.ds(pl.multiple_of(j * G, G), G)
-        lse_row = rows_to_lanes(lse_t[stat, :])
-        delta_row = rows_to_lanes(delta_t[stat, :])
-
-        def block_step(b, _):
-            at = pl.ds(pl.multiple_of(b * block, block), block)
-            slots = pl.ds(b * (block // rows), block // rows)
-
-            def keep(chunk, score_low):
-                score_grads[j, at, chunk] = score_low
-
-            dk, dv = part_grads(
-                gathered[0, slots, :, head].reshape(block, HD),
-                gathered[1, slots, :, head].reshape(block, HD),
-                head_pair(q_ref, j), head_pair(do_ref, j), lse_row, delta_row, None, keep,
-            )
-            use(slots, jnp.concatenate([dk, dv], 1).reshape(block // rows, rows, 2 * HD))
-            return 0
-
-        if prompt_rows == block:
-            block_step(0, 0)
-        else:
-            lax.fori_loop(0, prompt_rows // block, block_step, 0)
-
-    def cross_copy(i):
-        return pltpu.make_async_remote_copy(
-            src_ref=crossed.at[0, i],
-            dst_ref=crossed.at[1, i],
-            send_sem=cross_send.at[i],
-            recv_sem=cross_recv.at[i],
-            device_id=partner,
-            device_id_type=MESH,
-        )
-
-    def cross_step(i, _):
-        def use(slots, both):
-            crossed[0, i, slots] = both
-
-        prompt_head((1 - half) * heads + i, use)
-        cross_copy(i).start()
-        return 0
-
-    for i in range(heads):
-        cross_step(i, 0)
 
     def part_copy(i, d):
         return pltpu.make_async_remote_copy(
@@ -253,46 +216,83 @@
             device_id_type=MESH,
         )
 
-    def part_step(i, _):
-        cross_copy(i).wait_recv()
-
-        def use(slots, both):
-            parts[i, slots] = (both + crossed[1, i, slots]).astype(jnp.bfloat16)
-
-        prompt_head(half * heads + i, use)
+    def part_step(i):
+        head = slice(i * HD, (i + 1) * HD)
+        j = half * heads + i
+        own_stat = pl.ds(pl.multiple_of(j * G, G), G)
+        other_stat = slice(i * G, (i + 1) * G)
+        sides = (
+            (head_pair(q_ref, j), head_pair(do_ref, j), stats[0, own_stat], stats[1, own_stat]),
+            (
+                head_pair(q_other, i), head_pair(do_other, i),
+                stats_other[0, other_stat], stats_other[1, other_stat],
+            ),
+        )
+
+        def block_step(b, _):
+            at = pl.ds(pl.multiple_of(b * block, block), block)
+            slots = pl.ds(b * (block // rows), block // rows)
+            keys = gathered[slots, 0, :, head].reshape(block, HD)
+            values = gathered[slots, 1, :, head].reshape(block, HD)
+            both = None
+            for side, (queries, grads, lse, delta) in enumerate(sides):
+
+                def keep(chunk, score_low):
+                    prompt_low[side, i, at, chunk] = score_low
+
+                dk, dv = part_grads(
+                    keys, values, queries, grads, rows_to_lanes(lse), rows_to_lanes(delta), None,
+                    keep,
+                )
+                term = jnp.concatenate([dk, dv], 1)
+                both = term if both is None else both + term
+            parts[i, slots] = both.astype(jnp.bfloat16).reshape(block // rows, rows, 2 * HD)
+            return 0
+
+        if prompt_rows == block:
+            block_step(0, 0)
+        else:
+            lax.fori_loop(0, prompt_rows // block, block_step, 0)
 
         def start_part(d, _):
             part_copy(i, d).start()
             return 0
 
         lax.fori_loop(1, n, start_part, 0)
-        return 0
 
     for i in range(heads):
-        part_step(i, 0)
-
-    def query_step(j, _):
-        head = pl.ds(pl.multiple_of(j * HD, HD), HD)
-        keys = jnp.concatenate(
-            [gathered[0, :, :, head].reshape(prompt_rows, HD), k_ref[:, head]], 0
-        )
-        dq_t = (dot(keys.T, score_grads[j]) * SCALE).astype(jnp.bfloat16)
+        part_step(i)
+
+    def back_copy(i):
+        return pltpu.make_async_remote_copy(
+            src_ref=dq_other.at[0, i],
+            dst_ref=dq_other.at[1, i],
+            send_sem=back_send.at[i],
+            recv_sem=back_recv.at[i],
+            device_id=partner,
+            device_id_type=MESH,
+        )
+
+    def prompt_term(side, i):
+        keys = gathered[:, 0, :, i * HD : (i + 1) * HD].reshape(prompt_rows, HD)
+        return dot(keys.T, prompt_low[side, i])
+
+    def store_queries(j, prompt_sum):
+        keys = k_ref[:, pl.ds(pl.multiple_of(j * HD, HD), HD)]
+        dq_t = ((prompt_sum + dot(keys.T, own_low[j])) * SCALE).astype(jnp.bfloat16)
         for g in range(G):
             at = pl.ds(pl.multiple_of((j * G + g) * HD, HD), HD)
             dq_ref[:, at] = dq_t[:, g * HD : (g + 1) * HD].T
-        return 0
-
-    lax.fori_loop(0, KVH, query_step, 0)
+
+    for i in range(heads):
+        dq_other[0, i] = prompt_term(1, i)
+        back_copy(i).start()
+    for i in range(heads):
+        store_queries(half * heads + i, prompt_term(0, i))
+    for i in range(heads):
+        back_copy(i).wait()
+        store_queries((1 - half) * heads + i, dq_other[1, i])
     stores[2].start()
-
-    def end_sends(d, _):
-        gather_copy(d).wait_send()
-        pass_copy(d).wait_send()
-        return 0
-
-    lax.fori_loop(1, n, end_sends, 0)
-    for i in range(heads):
-        cross_copy(i).wait_send()
 
     def sum_step(i, _):
         def wait_part(d, _):
@@ -381,11 +381,14 @@
             pltpu.VMEM((tokens, q_width), bf16),
             pltpu.VMEM((H, tokens), f32),
             pltpu.VMEM((tokens, q_width), bf16),
-            pltpu.VMEM((H, tokens), f32),
-            pltpu.VMEM((HD, tokens), f32),
-            pltpu.VMEM((KVH, n * rows + tokens, G * tokens), bf16),
-            pltpu.VMEM((2, n, rows, width), bf16),
-            pltpu.VMEM((2, heads, n, rows, 2 * HD), f32),
+            pltpu.VMEM((2, H, tokens), f32),
+            pltpu.VMEM((KVH, tokens, G * tokens), bf16),
+            pltpu.VMEM((2, heads, n * rows, G * tokens), bf16),
+            pltpu.VMEM((tokens, q_width // 2), bf16),
+            pltpu.VMEM((tokens, q_width // 2), bf16),
+            pltpu.VMEM((2, H // 2, tokens), f32),
+            pltpu.VMEM((2, heads, HD, G * tokens), f32),
+            pltpu.VMEM((n, 2, rows, heads * HD), bf16),
             pltpu.VMEM((heads, n, rows, 2 * HD), bf16),
             pltpu.VMEM((heads, n, rows, 2 * HD), bf16),
             pltpu.VMEM((ns, heads, rows, 2 * HD), f32),
@@ -393,8 +396,8 @@
             dma((3,)),
             dma((n,)),
             dma((n,)),
-            dma((n,)),
-            dma((n,)),
+            dma((3,)),
+            dma((3,)),
             dma((heads,)),
             dma((heads,)),
             dma((heads, n)),

time: 31.5 us -> 27.8 us (0.88)
  Pallas kernels: 30.1 us -> 26.3 us
    pallas_call x1, Pallas kernels: 28.9 us -> 25.2 us  [body(): pl.pallas_call(functools.partial(kernel, n, ns, rows), out_shape=tuple((p...]
where the time goes in v6:
time: 27.8 us; the launch traced here: 27.6 us
  Pallas kernels  26.3 us (95%)
  between operations  1.29 us (5%)
    pallas_call x1, Pallas kernels, body(): pl.pallas_call(functools.partial(kernel, n, ns, rows), out_shape=tuple((p...  25.2 us
    pallas_call x1, Pallas kernels, body(): pl.pallas_call(store_kernel, out_shape=out_shape, in_specs=[vmem] * 5, ou...  1.1 us

profile of v6, /device:TPU:0, one launch (start us, length us, event | category | flops | bytes accessed | tf_op | source)
XLA Modules:
  0.0 27.6 jit_solution(9945213111295748764)
XLA Ops:
  1.3 25.2 %shard_map.128 = (bf16[1,128,4096]{2,1,0:T(8,128)(2,1)S(1)}, bf16[1,128,512]{2,1,0:T(8,128)(2,1)S(1)}, bf16[1,128,512]{2,1,0:T(8,128)(2,1)S(1)}, f32[16,512]{1,0:T(8,128)S(1)}, f32[16,512]{1,0:T(8,128)S(1)}) custom-call(s32[1]{0:T(128)S(6)} %copy.14.length_hbm, bf16[1,128,4096]{2,1,0:T(8,128)(2,1)} %q_hbm.1, bf16[1,128,512]{2,1,0:T(8,128)(2,1)} %k_hbm.1, ...), custom_call_target="tpu_custom_call" | custom-call | flops 2000000000 | bytes 5000000 | tf_op jit(solution)/shard_map/pallas_call | solution.py:368
  26.5 1.1 %shard_map.129 = (bf16[1,128,4096]{2,1,0:T(8,128)(2,1)}, bf16[1,128,512]{2,1,0:T(8,128)(2,1)}, bf16[1,128,512]{2,1,0:T(8,128)(2,1)}, f32[16,512]{1,0:T(8,128)}, f32[16,512]{1,0:T(8,128)}) custom-call(bf16[1,128,4096]{2,1,0:T(8,128)(2,1)S(1)} %get-tuple-element.10.refs_0_, bf16[1,128,512]{2,1,0:T(8,128)(2,1)S(1)} %get-tuple-element.11.refs_1_, ...), custom_call_target="tpu_custom_call" | custom-call | tf_op jit(solution)/shard_map/pallas_call | solution.py:415

commit v7 on v6

--- a/solution.py
+++ b/solution.py
@@ -67,11 +67,11 @@
 
 def kernel(
     n, ns, rows, length_hbm, q_hbm, k_hbm, v_hbm, do_hbm, out_hbm, lse_hbm, pk_hbm, pv_hbm,
-    dq_hbm, dk_hbm, dv_hbm, pdk_ref, pdv_ref,
-    dk_ref, dv_ref, length_ref, q_ref, k_ref, v_ref, do_ref, out_ref, lse_ref, dq_ref,
+    dq_ref, dk_ref, dv_ref, pdk_ref, pdv_ref,
+    length_ref, q_ref, k_ref, v_ref, do_ref, out_ref, lse_ref,
     stats, own_low, prompt_low, q_other, do_other, stats_other, dq_other,
     gathered, parts, landed, totals,
-    load_sem, store_sem, gather_send, gather_recv, swap_send, swap_recv, back_send, back_recv,
+    load_sem, gather_send, gather_recv, swap_send, swap_recv, back_send, back_recv,
     part_send, part_recv, total_send, total_recv,
 ):
     tokens = q_ref.shape[0]
@@ -170,7 +170,8 @@
     stats[1] = deltas.T[:H]
     swaps[2].start()
 
-    def own_step(j, _):
+    def own_step(i, _):
+        j = lax.rem(half * heads + i, KVH)
         head = pl.ds(pl.multiple_of(j * HD, HD), HD)
         stat = pl.ds(pl.multiple_of(j * G, G), G)
         lse_row = rows_to_lanes(stats[0, stat, :])
@@ -183,18 +184,11 @@
             k_ref[:, head], v_ref[:, head], head_pair(q_ref, j), head_pair(do_ref, j),
             lse_row, delta_row, jnp.concatenate([causal] * 2, 1), keep,
         )
-        dk_ref[:, head] = dk.astype(jnp.bfloat16)
-        dv_ref[:, head] = dv.astype(jnp.bfloat16)
-        return 0
-
-    lax.fori_loop(0, KVH, own_step, 0)
-    stores = [
-        pltpu.make_async_copy(dk_ref, dk_hbm.at[0], store_sem.at[0]),
-        pltpu.make_async_copy(dv_ref, dv_hbm.at[0], store_sem.at[1]),
-        pltpu.make_async_copy(dq_ref, dq_hbm.at[0], store_sem.at[2]),
-    ]
-    stores[0].start()
-    stores[1].start()
+        dk_ref[0, :, head] = dk.astype(jnp.bfloat16)
+        dv_ref[0, :, head] = dv.astype(jnp.bfloat16)
+        return 0
+
+    lax.fori_loop(0, KVH - 1, own_step, 0)
 
     def end_gather(d, _):
         gather_copy(d).wait()
@@ -282,18 +276,17 @@
         dq_t = ((prompt_sum + dot(keys.T, own_low[j])) * SCALE).astype(jnp.bfloat16)
         for g in range(G):
             at = pl.ds(pl.multiple_of((j * G + g) * HD, HD), HD)
-            dq_ref[:, at] = dq_t[:, g * HD : (g + 1) * HD].T
+            dq_ref[0, :, at] = dq_t[:, g * HD : (g + 1) * HD].T
 
     for i in range(heads):
         dq_other[0, i] = prompt_term(1, i)
         back_copy(i).start()
+    own_step(KVH - 1, 0)
     for i in range(heads):
         store_queries(half * heads + i, prompt_term(0, i))
     for i in range(heads):
         back_copy(i).wait()
         store_queries((1 - half) * heads + i, dq_other[1, i])
-    stores[2].start()
-
     def sum_step(i, _):
         def wait_part(d, _):
             part_copy(i, d).wait()
@@ -326,8 +319,6 @@
             both = both + totals[s, j % heads]
         pdk_ref[:, j * HD : (j + 1) * HD] = both[:, :HD]
         pdv_ref[:, j * HD : (j + 1) * HD] = both[:, HD:]
-    for store in stores:
-        store.wait()
 
 
 def store_kernel(*refs):
@@ -351,7 +342,6 @@
     heads = KVH // 2
     vmem = pl.BlockSpec(memory_space=pltpu.VMEM)
     hbm = pl.BlockSpec(memory_space=pltpu.HBM)
-    free = pl.BlockSpec(memory_space=pl.ANY)
     dma = pltpu.SemaphoreType.DMA
     out_shape = (
         jax.ShapeDtypeStruct(resp_q.shape, bf16),
@@ -369,10 +359,8 @@
         functools.partial(kernel, n, ns, rows),
         out_shape=tuple(pltpu.VMEM(o.shape, o.dtype) for o in out_shape),
         in_specs=[hbm] * 9,
-        out_specs=(free, free, free, vmem, vmem),
+        out_specs=(vmem,) * 5,
         scratch_shapes=[
-            pltpu.VMEM((tokens, width), bf16),
-            pltpu.VMEM((tokens, width), bf16),
             pltpu.SMEM((1,), jnp.int32),
             pltpu.VMEM((tokens, q_width), bf16),
             pltpu.VMEM((tokens, width), bf16),
@@ -380,7 +368,6 @@
             pltpu.VMEM((tokens, q_width), bf16),
             pltpu.VMEM((tokens, q_width), bf16),
             pltpu.VMEM((H, tokens), f32),
-            pltpu.VMEM((tokens, q_width), bf16),
             pltpu.VMEM((2, H, tokens), f32),
             pltpu.VMEM((KVH, tokens, G * tokens), bf16),
             pltpu.VMEM((2, heads, n * rows, G * tokens), bf16),
@@ -393,7 +380,6 @@
             pltpu.VMEM((heads, n, rows, 2 * HD), bf16),
             pltpu.VMEM((ns, heads, rows, 2 * HD), f32),
             dma((9,)),
-            dma((3,)),
             dma((n,)),
             dma((n,)),
             dma((3,)),

time: 27.8 us -> 27.7 us (level)
  no operation moved by 1% of the time
where the time goes in v7:
time: 27.7 us; the launch traced here: 27.6 us
  Pallas kernels  26.3 us (95%)
  between operations  1.29 us (5%)
    pallas_call x1, Pallas kernels, body(): pl.pallas_call(functools.partial(kernel, n, ns, rows), out_shape=tuple((p...  25.2 us
    pallas_call x1, Pallas kernels, body(): pl.pallas_call(store_kernel, out_shape=out_shape, in_specs=[vmem] * 5, ou...  1.1 us

profile of v7, /device:TPU:0, one launch (start us, length us, event | category | flops | bytes accessed | tf_op | source)
XLA Modules:
  0.0 27.6 jit_solution(13602779823064965778)
XLA Ops:
  1.3 25.2 %shard_map.128 = (bf16[1,128,4096]{2,1,0:T(8,128)(2,1)S(1)}, bf16[1,128,512]{2,1,0:T(8,128)(2,1)S(1)}, bf16[1,128,512]{2,1,0:T(8,128)(2,1)S(1)}, f32[16,512]{1,0:T(8,128)S(1)}, f32[16,512]{1,0:T(8,128)S(1)}) custom-call(s32[1]{0:T(128)S(6)} %copy.14.length_hbm, bf16[1,128,4096]{2,1,0:T(8,128)(2,1)} %q_hbm.1, bf16[1,128,512]{2,1,0:T(8,128)(2,1)} %k_hbm.1, ...), custom_call_target="tpu_custom_call" | custom-call | flops 2000000000 | bytes 5000000 | tf_op jit(solution)/shard_map/pallas_call | solution.py:358
  26.5 1.1 %shard_map.129 = (bf16[1,128,4096]{2,1,0:T(8,128)(2,1)}, bf16[1,128,512]{2,1,0:T(8,128)(2,1)}, bf16[1,128,512]{2,1,0:T(8,128)(2,1)}, f32[16,512]{1,0:T(8,128)}, f32[16,512]{1,0:T(8,128)}) custom-call(bf16[1,128,4096]{2,1,0:T(8,128)(2,1)S(1)} %get-tuple-element.10.refs_0_, bf16[1,128,512]{2,1,0:T(8,128)(2,1)S(1)} %get-tuple-element.11.refs_1_, ...), custom_call_target="tpu_custom_call" | custom-call | tf_op jit(solution)/shard_map/pallas_call | solution.py:401

commit v8 on v7

--- a/solution.py
+++ b/solution.py
@@ -284,9 +284,6 @@
     own_step(KVH - 1, 0)
     for i in range(heads):
         store_queries(half * heads + i, prompt_term(0, i))
-    for i in range(heads):
-        back_copy(i).wait()
-        store_queries((1 - half) * heads + i, dq_other[1, i])
     def sum_step(i, _):
         def wait_part(d, _):
             part_copy(i, d).wait()
@@ -311,6 +308,9 @@
 
     for d in range(1, ns):
         total_copy(d).start()
+    for i in range(heads):
+        back_copy(i).wait()
+        store_queries((1 - half) * heads + i, dq_other[1, i])
     for d in range(1, ns):
         total_copy(d).wait()
     for j in range(KVH):

time: 27.7 us -> 27.8 us (level)
  no operation moved by 1% of the time
where the time goes in v8:
time: 27.8 us; the launch traced here: 27.6 us
  Pallas kernels  26.3 us (95%)
  between operations  1.29 us (5%)
    pallas_call x1, Pallas kernels, body(): pl.pallas_call(functools.partial(kernel, n, ns, rows), out_shape=tuple((p...  25.2 us
    pallas_call x1, Pallas kernels, body(): pl.pallas_call(store_kernel, out_shape=out_shape, in_specs=[vmem] * 5, ou...  1.1 us

profile of v8, /device:TPU:0, one launch (start us, length us, event | category | flops | bytes accessed | tf_op | source)
XLA Modules:
  0.0 27.6 jit_solution(13703844444185106456)
XLA Ops:
  1.3 25.2 %shard_map.128 = (bf16[1,128,4096]{2,1,0:T(8,128)(2,1)S(1)}, bf16[1,128,512]{2,1,0:T(8,128)(2,1)S(1)}, bf16[1,128,512]{2,1,0:T(8,128)(2,1)S(1)}, f32[16,512]{1,0:T(8,128)S(1)}, f32[16,512]{1,0:T(8,128)S(1)}) custom-call(s32[1]{0:T(128)S(6)} %copy.14.length_hbm, bf16[1,128,4096]{2,1,0:T(8,128)(2,1)} %q_hbm.1, bf16[1,128,512]{2,1,0:T(8,128)(2,1)} %k_hbm.1, ...), custom_call_target="tpu_custom_call" | custom-call | flops 2000000000 | bytes 5000000 | tf_op jit(solution)/shard_map/pallas_call | solution.py:358
  26.5 1.1 %shard_map.129 = (bf16[1,128,4096]{2,1,0:T(8,128)(2,1)}, bf16[1,128,512]{2,1,0:T(8,128)(2,1)}, bf16[1,128,512]{2,1,0:T(8,128)(2,1)}, f32[16,512]{1,0:T(8,128)}, f32[16,512]{1,0:T(8,128)}) custom-call(bf16[1,128,4096]{2,1,0:T(8,128)(2,1)S(1)} %get-tuple-element.10.refs_0_, bf16[1,128,512]{2,1,0:T(8,128)(2,1)S(1)} %get-tuple-element.11.refs_1_, ...), custom_call_target="tpu_custom_call" | custom-call | tf_op jit(solution)/shard_map/pallas_call | solution.py:401
